TPU v7x, 32 devices: a whole 2x2x4 slice. The times are simulated.
32 devices in a mesh: dp: 8 (over z, x), fsdp: 4 (over y, core).
Axes of the slice: x: 2, y: 2, z: 4, core: 2. Of those that a mesh axis runs over, the one named last changes fastest.
Arguments:
- tokens: bfloat16 [65536, 1024], P(('dp', 'fsdp')), may hold values from -6 to 6
- in_weight: bfloat16 [1024, 4384], P(('dp', 'fsdp')), may hold values from -0.1875 to 0.1875
- out_weight: bfloat16 [2048, 1024], P(None, ('dp', 'fsdp')), may hold values from -0.125 to 0.125
- conv_weight: bfloat16 [4, 2304], P(None, ('dp', 'fsdp')), may hold values from -3 to 3
- conv_bias: bfloat16 [2304], P(('dp', 'fsdp')), may hold values from -0.5 to 0.5
- norm_gain: bfloat16 [1024], P(('dp', 'fsdp')), may hold values from 0.5 to 1.5
- gate_gain: bfloat16 [2048], P(('dp', 'fsdp')), may hold values from 0.5 to 1.5
- decay_log: float32 [32], P('fsdp'), may hold values from 0 to 2.77
- step_bias: float32 [32], P('fsdp'), may hold values from -6.5 to -2.5
- skip_scale: float32 [32], P('fsdp'), may hold values from 0.5 to 1.5
- cotangent: bfloat16 [65536, 1024], P(('dp', 'fsdp')), may hold values from -6 to 6
Outputs:
- out_tokens: bfloat16 [65536, 1024], P(('dp', 'fsdp'))
- token_grad: bfloat16 [65536, 1024], P(('dp', 'fsdp'))
- in_weight_grad: float32 [1024, 4384], P(('dp', 'fsdp'))
- out_weight_grad: float32 [2048, 1024], P(None, ('dp', 'fsdp'))
- conv_weight_grad: float32 [4, 2304], P(None, ('dp', 'fsdp'))
- conv_bias_grad: float32 [2304], P(('dp', 'fsdp'))
- norm_gain_grad: float32 [1024], P(('dp', 'fsdp'))
- gate_gain_grad: float32 [2048], P(('dp', 'fsdp'))
- decay_log_grad: float32 [32], P('fsdp')
- step_bias_grad: float32 [32], P('fsdp')
- skip_scale_grad: float32 [32], P('fsdp')
All inputs are finite; a program needn't handle non-finite values.
Results may differ from a plain program's by a relative error of at most 0.0095.
Values may be sent and summed in bfloat16 or wider, within the bound.
A program may use at most 384 MiB of HBM per device.

v0:
```python
import jax
import jax.numpy as jnp
from jax import lax
from jax.sharding import PartitionSpec as P

HEADS = 32
HEADDIM = 64
STATE = 128
KCONV = 4
GROUP = 256
SEQ_LEN = 1024
INNER = 2048
CONVDIM = 2304


EPSILON = 1e-05


def silu_slope(pre_act):
    logistic = jax.nn.sigmoid(pre_act)
    return logistic * (1.0 + pre_act * (1.0 - logistic))


def forward_pass(tokens, weights, head_params):
    in_weight, out_weight, conv_weight, conv_bias, norm_gain, gate_gain = weights
    decay_log, step_bias, skip_scale = head_params
    seq_count = tokens.shape[0] // SEQ_LEN
    groups = SEQ_LEN // GROUP
    inputs = tokens.astype(jnp.float32)
    norm_scale = lax.rsqrt(jnp.mean(inputs * inputs, axis=-1, keepdims=True) + EPSILON)
    normed = (inputs * norm_scale * norm_gain.astype(jnp.float32)).astype(jnp.bfloat16)
    projected = jnp.dot(normed, in_weight, preferred_element_type=jnp.float32)
    gate_in = projected[:, :INNER]
    conv_in = projected[:, INNER : INNER + CONVDIM].reshape(seq_count, SEQ_LEN, CONVDIM)
    step_raw = projected[:, INNER + CONVDIM :]
    padded = jnp.pad(conv_in, ((0, 0), (KCONV - 1, 0), (0, 0)))
    conv_float = conv_weight.astype(jnp.float32)
    pre_act = conv_bias.astype(jnp.float32) + sum(
        (
            conv_float[conv_tap] * padded[:, conv_tap : conv_tap + SEQ_LEN]
            for conv_tap in range(KCONV)
        )
    )
    active = jax.nn.silu(pre_act)
    values = active[..., :INNER].reshape(seq_count, groups, GROUP, HEADS, HEADDIM)
    values_low = values.astype(jnp.bfloat16)
    b_low = (
        active[..., INNER : INNER + STATE]
        .reshape(seq_count, groups, GROUP, STATE)
        .astype(jnp.bfloat16)
    )
    c_low = (
        active[..., INNER + STATE :].reshape(seq_count, groups, GROUP, STATE).astype(jnp.bfloat16)
    )
    step_size = jax.nn.softplus(step_raw + step_bias)
    decay_rate = -jnp.exp(decay_log)
    step_heads = jnp.moveaxis(step_size.reshape(seq_count, groups, GROUP, HEADS), 3, 2)
    cumulated = jnp.cumsum(step_heads * decay_rate[:, None], axis=-1)
    row_ids = lax.broadcasted_iota(jnp.int32, (GROUP, GROUP), 0)
    col_ids = lax.broadcasted_iota(jnp.int32, (GROUP, GROUP), 1)
    causal = row_ids >= col_ids
    differ = cumulated[..., :, None] - cumulated[..., None, :]
    decay_table = jnp.where(causal, jnp.exp(jnp.where(causal, differ, 0.0)), 0.0)
    gram_matrix = jnp.einsum("bcqn,bcsn->bcqs", c_low, b_low, preferred_element_type=jnp.float32)
    mixing = (gram_matrix[:, :, None] * decay_table * step_heads[..., None, :]).astype(jnp.bfloat16)
    intra_out = jnp.einsum(
        "bchqs,bcshp->bcqhp", mixing, values_low, preferred_element_type=jnp.float32
    )
    last_cum = cumulated[..., -1:]
    weight_s = jnp.exp(last_cum - cumulated) * step_heads
    scaled_b = (weight_s[..., None] * b_low[:, :, None]).astype(jnp.bfloat16)
    group_state = jnp.einsum(
        "bchsn,bcshp->bchnp", scaled_b, values_low, preferred_element_type=jnp.float32
    )
    group_decay = jnp.exp(last_cum[..., 0])
    carried = jnp.zeros((seq_count, HEADS, STATE, HEADDIM), jnp.float32)
    entering_list = []
    for group_index in range(groups):
        entering_list.append(carried)
        carried = group_decay[:, group_index, :, None, None] * carried + group_state[:, group_index]
    entering = jnp.stack(entering_list, axis=1)
    entering_low = entering.astype(jnp.bfloat16)
    inter_raw = jnp.einsum(
        "bcqn,bchnp->bcqhp", c_low, entering_low, preferred_element_type=jnp.float32
    )
    growth = jnp.exp(jnp.moveaxis(cumulated, 2, 3))
    inter_out = growth[..., None] * inter_raw
    ssm_out = (intra_out + inter_out + skip_scale[:, None] * values).reshape(-1, INNER)
    silu_gate = jax.nn.silu(gate_in)
    gated_out = ssm_out * silu_gate
    gate_scale = lax.rsqrt(jnp.mean(gated_out * gated_out, axis=-1, keepdims=True) + EPSILON)
    mixed_low = (gated_out * gate_scale * gate_gain.astype(jnp.float32)).astype(jnp.bfloat16)
    output = inputs + jnp.dot(mixed_low, out_weight, preferred_element_type=jnp.float32)
    stored = {
        "inputs": inputs,
        "norm_scale": norm_scale,
        "normed": normed,
        "gate_in": gate_in,
        "step_raw": step_raw,
        "padded": padded,
        "pre_act": pre_act,
        "values": values,
        "values_low": values_low,
        "b_low": b_low,
        "c_low": c_low,
        "step_heads": step_heads,
        "decay_rate": decay_rate,
        "cumulated": cumulated,
        "decay_table": decay_table,
        "gram_matrix": gram_matrix,
        "mixing": mixing,
        "weight_s": weight_s,
        "scaled_b": scaled_b,
        "group_decay": group_decay,
        "entering": entering,
        "entering_low": entering_low,
        "growth": growth,
        "inter_out": inter_out,
        "ssm_out": ssm_out,
        "silu_gate": silu_gate,
        "gated_out": gated_out,
        "gate_scale": gate_scale,
        "mixed_low": mixed_low,
    }
    return (output.astype(jnp.bfloat16), stored)


def output_side(cotangent, weights, stored):
    out_weight = weights[1]
    gate_gain = weights[5]
    out_weight_grad = jnp.einsum(
        "ti,td->id", stored["mixed_low"], cotangent, preferred_element_type=jnp.float32
    )
    mixed_grad = jnp.einsum("td,id->ti", cotangent, out_weight, preferred_element_type=jnp.float32)
    gated_out = stored["gated_out"]
    gate_scale = stored["gate_scale"]
    gate_gain_grad = jnp.sum(mixed_grad * gated_out * gate_scale, axis=0)
    scaled_in = mixed_grad * gate_gain.astype(jnp.float32)
    gated_grad = gate_scale * (
        scaled_in
        - gated_out
        * gate_scale
        * gate_scale
        * jnp.mean(scaled_in * gated_out, axis=-1, keepdims=True)
    )
    ssm_grad = (gated_grad * stored["silu_gate"]).astype(jnp.bfloat16)
    gate_grad = gated_grad * stored["ssm_out"] * silu_slope(stored["gate_in"])
    return (out_weight_grad, gate_gain_grad, ssm_grad, gate_grad)


def mixer_side(ssm_grad, gate_grad, cotangent, weights, head_params, stored):
    in_weight, out_weight, conv_weight, conv_bias, norm_gain, gate_gain = weights
    decay_log, step_bias, skip_scale = head_params
    values = stored["values"]
    values_low = stored["values_low"]
    b_low = stored["b_low"]
    c_low = stored["c_low"]
    step_heads = stored["step_heads"]
    decay_rate = stored["decay_rate"]
    cumulated = stored["cumulated"]
    gram_matrix = stored["gram_matrix"]
    weight_s = stored["weight_s"]
    group_decay = stored["group_decay"]
    entering = stored["entering"]
    seq_count = values.shape[0]
    groups = values.shape[1]
    ssm_grad = ssm_grad.reshape(seq_count, groups, GROUP, HEADS, HEADDIM)
    skip_grad = jnp.sum(ssm_grad * values, axis=(0, 1, 2, 4))
    values_grad = skip_scale[:, None] * ssm_grad
    values_grad = values_grad + jnp.einsum(
        "bchqs,bcqhp->bcshp", stored["mixing"], ssm_grad, preferred_element_type=jnp.float32
    )
    mixing_grad = jnp.einsum(
        "bcqhp,bcshp->bchqs", ssm_grad, values_low, preferred_element_type=jnp.float32
    )
    through = mixing_grad * stored["decay_table"]
    gram_grad = jnp.sum(through * step_heads[..., None, :], axis=2).astype(jnp.bfloat16)
    along = through * gram_matrix[:, :, None]
    step_grad = jnp.sum(along, axis=3)
    along = along * step_heads[..., None, :]
    cum_grad = jnp.sum(along, axis=4) - jnp.sum(along, axis=3)
    b_grad = jnp.einsum("bcqs,bcqn->bcsn", gram_grad, c_low, preferred_element_type=jnp.float32)
    c_grad = jnp.einsum("bcqs,bcsn->bcqn", gram_grad, b_low, preferred_element_type=jnp.float32)
    raw_grad = (stored["growth"][..., None] * ssm_grad).astype(jnp.bfloat16)
    cum_grad = cum_grad + jnp.moveaxis(jnp.sum(ssm_grad * stored["inter_out"], axis=-1), 2, 3)
    entering_grad = jnp.einsum(
        "bcqn,bcqhp->bchnp", c_low, raw_grad, preferred_element_type=jnp.float32
    )
    c_grad = c_grad + jnp.einsum(
        "bcqhp,bchnp->bcqn", raw_grad, stored["entering_low"], preferred_element_type=jnp.float32
    )
    running = jnp.zeros_like(entering[:, 0])
    state_list = []
    decay_list = []
    for group_index in reversed(range(groups)):
        state_list.insert(0, running)
        decay_list.insert(0, jnp.sum(running * entering[:, group_index], axis=(2, 3)))
        running = (
            entering_grad[:, group_index] + group_decay[:, group_index, :, None, None] * running
        )
    state_grad = jnp.stack(state_list, axis=1).astype(jnp.bfloat16)
    decay_grad = jnp.stack(decay_list, axis=1)
    scaled_grad = jnp.einsum(
        "bcshp,bchnp->bchsn", values_low, state_grad, preferred_element_type=jnp.float32
    )
    values_grad = values_grad + jnp.einsum(
        "bchsn,bchnp->bcshp", stored["scaled_b"], state_grad, preferred_element_type=jnp.float32
    )
    b_grad = b_grad + jnp.sum(scaled_grad * weight_s[..., None], axis=2)
    weight_grad = jnp.sum(scaled_grad * b_low[:, :, None], axis=-1)
    fading = jnp.exp(cumulated[..., -1:] - cumulated)
    step_grad = step_grad + weight_grad * fading
    weight_term = weight_grad * weight_s
    last_grad = jnp.sum(weight_term, axis=-1) + decay_grad * group_decay
    cum_grad = cum_grad - weight_term
    cum_grad = cum_grad.at[..., -1].add(last_grad)
    rate_grad = jnp.flip(jnp.cumsum(jnp.flip(cum_grad, -1), axis=-1), -1)
    step_grad = step_grad + rate_grad * decay_rate[:, None]
    decay_log_grad = jnp.sum(rate_grad * step_heads, axis=(0, 1, 3)) * decay_rate
    step_rows = jnp.moveaxis(step_grad, 2, 3).reshape(-1, HEADS)
    step_raw_grad = step_rows * jax.nn.sigmoid(stored["step_raw"] + step_bias)
    step_bias_grad = jnp.sum(step_raw_grad, axis=0)
    active_grad = jnp.concatenate(
        [
            values_grad.reshape(seq_count, SEQ_LEN, INNER),
            b_grad.reshape(seq_count, SEQ_LEN, STATE),
            c_grad.reshape(seq_count, SEQ_LEN, STATE),
        ],
        axis=-1,
    )
    pre_grad = active_grad * silu_slope(stored["pre_act"])
    conv_bias_grad = jnp.sum(pre_grad, axis=(0, 1))
    padded = stored["padded"]
    conv_weight_grad = jnp.stack(
        [
            jnp.sum(pre_grad * padded[:, conv_tap : conv_tap + SEQ_LEN], axis=(0, 1))
            for conv_tap in range(KCONV)
        ]
    )
    grad_padded = jnp.pad(pre_grad, ((0, 0), (0, KCONV - 1), (0, 0)))
    conv_float = conv_weight.astype(jnp.float32)
    conv_in_grad = sum(
        (
            conv_float[conv_tap]
            * grad_padded[:, KCONV - 1 - conv_tap : KCONV - 1 - conv_tap + SEQ_LEN]
            for conv_tap in range(KCONV)
        )
    )
    proj_grad = jnp.concatenate(
        [gate_grad, conv_in_grad.reshape(-1, CONVDIM), step_raw_grad], axis=-1
    ).astype(jnp.bfloat16)
    in_weight_grad = jnp.einsum(
        "td,te->de", stored["normed"], proj_grad, preferred_element_type=jnp.float32
    )
    normed_grad = jnp.einsum("te,de->td", proj_grad, in_weight, preferred_element_type=jnp.float32)
    inputs = stored["inputs"]
    norm_scale = stored["norm_scale"]
    norm_gain_grad = jnp.sum(normed_grad * inputs * norm_scale, axis=0)
    scaled_in = normed_grad * norm_gain.astype(jnp.float32)
    token_grad = norm_scale * (
        scaled_in
        - inputs * norm_scale * norm_scale * jnp.mean(scaled_in * inputs, axis=-1, keepdims=True)
    ) + cotangent.astype(jnp.float32)
    return (
        token_grad.astype(jnp.bfloat16),
        in_weight_grad,
        conv_weight_grad,
        conv_bias_grad,
        norm_gain_grad,
        decay_log_grad,
        step_bias_grad,
        skip_grad,
    )


def on_device(
    tokens,
    in_weight,
    out_weight,
    conv_weight,
    conv_bias,
    norm_gain,
    gate_gain,
    decay_log,
    step_bias,
    skip_scale,
    cotangent,
):
    weights = (
        lax.all_gather(in_weight, ("dp", "fsdp"), axis=0, tiled=True),
        lax.all_gather(out_weight, ("dp", "fsdp"), axis=1, tiled=True),
        lax.all_gather(conv_weight, ("dp", "fsdp"), axis=1, tiled=True),
        lax.all_gather(conv_bias, ("dp", "fsdp"), axis=0, tiled=True),
        lax.all_gather(norm_gain, ("dp", "fsdp"), axis=0, tiled=True),
        lax.all_gather(gate_gain, ("dp", "fsdp"), axis=0, tiled=True),
    )
    head_params = (
        lax.all_gather(decay_log, "fsdp", axis=0, tiled=True),
        lax.all_gather(step_bias, "fsdp", axis=0, tiled=True),
        lax.all_gather(skip_scale, "fsdp", axis=0, tiled=True),
    )
    output, stored = forward_pass(tokens, weights, head_params)
    weights = (
        lax.all_gather(in_weight, ("dp", "fsdp"), axis=0, tiled=True),
        lax.all_gather(out_weight, ("dp", "fsdp"), axis=1, tiled=True),
        lax.all_gather(conv_weight, ("dp", "fsdp"), axis=1, tiled=True),
        lax.all_gather(conv_bias, ("dp", "fsdp"), axis=0, tiled=True),
        lax.all_gather(norm_gain, ("dp", "fsdp"), axis=0, tiled=True),
        lax.all_gather(gate_gain, ("dp", "fsdp"), axis=0, tiled=True),
    )
    head_params = (
        lax.all_gather(decay_log, "fsdp", axis=0, tiled=True),
        lax.all_gather(step_bias, "fsdp", axis=0, tiled=True),
        lax.all_gather(skip_scale, "fsdp", axis=0, tiled=True),
    )
    out_weight_grad, gate_gain_grad, ssm_grad, gate_grad = output_side(cotangent, weights, stored)
    (
        token_grad,
        in_weight_grad,
        conv_weight_grad,
        conv_bias_grad,
        norm_gain_grad,
        decay_log_grad,
        step_bias_grad,
        skip_grad,
    ) = mixer_side(ssm_grad, gate_grad, cotangent, weights, head_params, stored)
    in_share, out_share, conv_weight_share, conv_bias_share, norm_share, gate_share = (
        lax.psum_scatter(in_weight_grad, ("dp", "fsdp"), scatter_dimension=0, tiled=True),
        lax.psum_scatter(out_weight_grad, ("dp", "fsdp"), scatter_dimension=1, tiled=True),
        lax.psum_scatter(conv_weight_grad, ("dp", "fsdp"), scatter_dimension=1, tiled=True),
        lax.psum_scatter(conv_bias_grad, ("dp", "fsdp"), scatter_dimension=0, tiled=True),
        lax.psum_scatter(norm_gain_grad, ("dp", "fsdp"), scatter_dimension=0, tiled=True),
        lax.psum_scatter(gate_gain_grad, ("dp", "fsdp"), scatter_dimension=0, tiled=True),
    )
    head_totals = lax.psum((decay_log_grad, step_bias_grad, skip_grad), ("dp", "fsdp"))
    head_share = decay_log.shape[0]
    first_head = lax.axis_index("fsdp") * head_share
    decay_share = lax.dynamic_slice_in_dim(head_totals[0], first_head, head_share)
    bias_share = lax.dynamic_slice_in_dim(head_totals[1], first_head, head_share)
    skip_share = lax.dynamic_slice_in_dim(head_totals[2], first_head, head_share)
    return (
        output,
        token_grad,
        in_share,
        out_share,
        conv_weight_share,
        conv_bias_share,
        norm_share,
        gate_share,
        decay_share,
        bias_share,
        skip_share,
    )


def solution(mesh):
    return jax.shard_map(
        on_device,
        mesh=mesh,
        in_specs=(
            P(("dp", "fsdp"), None),
            P(("dp", "fsdp"), None),
            P(None, ("dp", "fsdp")),
            P(None, ("dp", "fsdp")),
            P(("dp", "fsdp")),
            P(("dp", "fsdp")),
            P(("dp", "fsdp")),
            P("fsdp"),
            P("fsdp"),
            P("fsdp"),
            P(("dp", "fsdp"), None),
        ),
        out_specs=(
            P(("dp", "fsdp"), None),
            P(("dp", "fsdp"), None),
            P(("dp", "fsdp"), None),
            P(None, ("dp", "fsdp")),
            P(None, ("dp", "fsdp")),
            P(("dp", "fsdp")),
            P(("dp", "fsdp")),
            P(("dp", "fsdp")),
            P("fsdp"),
            P("fsdp"),
            P("fsdp"),
        ),
        check_vma=False,
    )
```

profile of v0, /device:TPU:0, one launch (start us, length us, event | category | flops | bytes accessed | tf_op | source)
XLA Modules:
  0.0 1005.9 jit_solution(9920433187809224039)
XLA Ops:
  11.3 43.3 %all-reduce.14 = (bf16[1024]{0:T(1024)(128)(2,1)S(1)}, bf16[2304]{0:T(1024)(128)(2,1)S(1)}, bf16[2048]{0:T(1024)(128)(2,1)S(1)}) all-reduce(bf16[1024]{0:T(1024)(128)(2,1)S(1)} %dynamic-update-slice.4, bf16[2304]{0:T(1024)(128)(2,1)S(1)} %dynamic-update-slice.3, ...), channel_id=1, replica_groups=mesh['dp'=8,'fsdp'=4] {'dp','fsdp'}, use_global_device_ids=true, to_apply=%add.3 | all-reduce | flops 5376 | bytes 21504
  54.6 3.1 fusion.32
  57.7 40.1 %all-gather = bf16[32,72,4]{1,2,0:T(4,128)(2,1)S(1)} all-gather(bf16[1,72,4]{1,2,0:T(4,128)(2,1)} %bitcast.234), channel_id=1, replica_groups=mesh['dp'=8,'fsdp'=4] {'dp','fsdp'}, dimensions={0}, use_global_device_ids=true | all-gather | bytes 19008 | tf_op jit(solution)/shard_map/all_gather | solution.py:292
  102.5 6.1 all-reduce.13
  109.2 27.7 %fusion.57 = f32[2048,4384]{0,1:T(8,128)} fusion(bf16[1024,4384]{1,0:T(8,128)(2,1)} %all-gather.4.cloned.1.call-done, bf16[2048,1024]{1,0:T(8,128)(2,1)} %param.13, f32[1024]{0:T(1024)S(1)} %convert_element_type.94, f32[2048]{0:T(1024)S(1)} %add_rsqrt_fusion.1), kind=kOutput, calls=%fused_computation.116 | convolution fusion | flops 18396217344 | bytes 49098752 | tf_op jit(solution)/shard_map/dot_general | solution.py:32
  136.9 15.3 %slice.168 = f32[2048,2304]{0,1:T(8,128)} slice(f32[2048,4384]{0,1:T(8,128)} %fusion.57), slice={[0:2048], [2048:4352]} | slice | bytes 37748736 | tf_op jit(solution)/shard_map/slice | solution.py:34
  154.5 4.6 reduce-window.14
  161.1 15.1 %copy.477 = f32[288,2,8,1024]{3,2,0,1:T(8,128)} copy(f32[288,2,8,1024]{3,2,1,0:T(8,128)} %bitcast.199) | data formatting | bytes 37748736 | tf_op jit(solution)/shard_map/reshape | solution.py:34
  176.2 43.9 %fusion.84 = (bf16[2,1024,2304]{1,2,0:T(8,128)(2,1)}, f32[2,1024,2304]{1,2,0:T(8,128)}, f32[2,1024,2304]{1,2,0:T(8,128)}) fusion(f32[2,1024,2304]{1,2,0:T(8,128)} %bitcast.197, f32[2304]{0:T(1024)S(1)} %get-tuple-element.46, f32[2304]{0:T(1024)S(1)} %get-tuple-element.47, f32[2304]{0:T(1024)S(1)} %get-tuple-element.48, f32[2304]{0:T(1024)S(1)} %get-tuple-element.45, ...), kind=kLoop, calls=%fused_computation.173 | loop fusion | flops 61341696 | bytes 66106368 | tf_op jit(solution)/shard_map/convert.14
  220.1 11.9 %slice.172 = f32[2,1024,2048]{1,2,0:T(8,128)} slice(f32[2,1024,2304]{1,2,0:T(8,128)} %get-tuple-element.70), slice={[0:2], [0:1024], [0:2048]} | slice | bytes 33554432 | tf_op jit(solution)/shard_map/slice | solution.py:45
  232.1 20.5 %reshape.203 = f32[2,4,256,32,64]{2,1,4,3,0:T(4,128)} reshape(f32[2,1024,2048]{1,2,0:T(8,128)} %slice.172) | data formatting | bytes 33554432 | tf_op jit(solution)/shard_map/reshape | solution.py:45
  252.6 2.1 fusion.86
  255.0 1.5 copy.360
  259.1 1.5 copy.369
  261.2 12.4 %fusion.4 = f32[2,4,32,128,64]{3,4,2,1,0:T(8,128)} fusion(f32[2,4,256,128]{2,3,1,0:T(8,128)} %copy.370, f32[2,4,32,256]{3,2,1,0:T(8,128)S(1)} %copy.369, f32[2,4,256,32,64]{2,1,4,3,0:T(4,128)} %reshape.203), kind=kOutput, calls=%fused_computation.16 | convolution fusion | flops 1090519040 | bytes 26476544 | tf_op jit(solution)/shard_map/bchsn,bcshp->bchnp/dot_general | solution.py:72
  273.6 3.6 fusion.65
  279.3 2.4 fusion.92
  281.7 2.0 fusion.91
  283.7 35.8 %fusion.18 = f32[2,4,256,32,64]{2,4,3,1,0:T(8,128)} fusion(f32[2,4,256,32,64]{2,1,4,3,0:T(4,128)} %reshape.203, f32[2,4,256,32,64]{2,4,3,1,0:T(8,128)S(1)} %bitcast.201, f32[32]{0:T(128)S(1)} %get-tuple-element.58, f32[2,4,256,32]{2,3,1,0:T(8,128)S(1)} %copy-done.19, f32[2,4,32,256]{3,2,1,0:T(8,128)S(1)} %copy.366, f32[2,4,32,256]{3,2,1,0:T(8,128)S(1)} %copy-done.21, ...), kind=kOutput, calls=%fused_computation.47 | convolution fusion | flops 2264924160 | bytes 53280896 | tf_op jit(solution)/shard_map/bchqs,bcshp->bcqhp/dot_general | solution.py:66
  319.5 20.9 %copy.377 = f32[2,4,256,32,64]{2,1,0,4,3:T(4,128)} copy(f32[2,4,256,32,64]{2,4,3,1,0:T(8,128)} %fusion.18) | data formatting | bytes 33554432 | tf_op jit(solution)/shard_map/add | solution.py:88
  340.4 20.7 %reshape.207 = f32[2048,2048]{0,1:T(8,128)} reshape(f32[2,4,256,32,64]{2,1,0,4,3:T(4,128)} %copy.377) | data formatting | bytes 33554432 | tf_op jit(solution)/shard_map/reshape | solution.py:88
  361.1 17.2 %multiply_reduce_fusion.12 = (f32[2048]{0:T(1024)S(1)}, f32[2048,2048]{0,1:T(8,128)}) fusion(f32[2048,2048]{0,1:T(8,128)} %reshape.207, f32[2048,4384]{0,1:T(8,128)} %fusion.57), kind=kLoop, calls=%fused_computation.54 | loop fusion | flops 29358080 | bytes 50339840 | tf_op jit(solution)/shard_map/reduce_sum | solution.py:91
  378.4 20.9 %multiply_reduce_fusion.10 = (f32[2048]{0:T(1024)}, f32[2048]{0:T(1024)S(1)}, f32[2048,2048]{0,1:T(8,128)}) fusion(f32[2048,2048]{0,1:T(8,128)} %get-tuple-element.68, f32[2048]{0:T(1024)S(1)} %add_rsqrt_fusion, f32[2048]{0:T(1024)S(1)} %copy-done.47, bf16[2048,1024]{1,0:T(8,128)(2,1)} %param.23, bf16[2048,1024]{0,1:T(8,128)(2,1)} %all-gather.6.cloned.1.call-done), kind=kOutput, calls=%fused_computation.48 | convolution fusion | flops 8615096320 | bytes 41975808 | tf_op jit(solution)/shard_map/td,id->ti/dot_general | solution.py:134
  399.4 35.1 %fusion.81 = (f32[2048,2048]{0,1:T(8,128)}, bf16[2048,2048]{0,1:T(8,128)(2,1)}, bf16[2048,2048]{0,1:T(8,128)(2,1)}) fusion(f32[2048,4384]{0,1:T(8,128)} %fusion.57, f32[2048]{0:T(1024)S(1)} %broadcast_multiply_fusion, f32[2048,2048]{0,1:T(8,128)} %get-tuple-element.68, f32[2048,2048]{0,1:T(8,128)} %get-tuple-element.91, f32[2048]{0:T(1024)S(1)} %copy-done.47, ...), kind=kLoop, calls=%fused_computation.171 | loop fusion | flops 83886080 | bytes 100687872 | tf_op jit(solution)/shard_map/convert_element_type | solution.py:169
  434.5 14.5 %reshape.208 = bf16[2,4,256,32,64]{2,1,0,4,3:T(4,128)(2,1)} reshape(bf16[2048,2048]{0,1:T(8,128)(2,1)} %get-tuple-element.63) | data formatting | bytes 16777216 | tf_op jit(solution)/shard_map/reshape | solution.py:167
  449.0 12.4 %fusion.16 = (f32[2,4,256,32]{2,3,1,0:T(8,128)}, bf16[2,4,256,32,64]{2,4,3,1,0:T(8,128)(2,1)S(1)}) fusion(f32[2,4,256,2048]{2,3,1,0} %copy-done, f32[2,4,256,32]{2,3,1,0:T(8,128)S(1)} %copy-done.19, bf16[2,4,256,32,64]{2,1,0,4,3:T(4,128)(2,1)} %reshape.208), kind=kLoop, calls=%fused_computation.43 | loop fusion | flops 25100288 | bytes 34078720 | tf_op jit(solution)/shard_map/reduce_sum | solution.py:185
  461.4 50.6 %multiply_reduce_fusion.1 = (f32[2,4,32,256]{3,2,1,0:T(8,128)}, f32[2,4,32,256]{3,2,1,0:T(8,128)}, f32[2,4,32,256]{3,2,1,0:T(8,128)}, bf16[2,4,256,256]{3,2,1,0:T(8,128)(2,1)}) fusion(f32[2,4,32,256]{3,2,1,0:T(8,128)S(1)} %copy-done.31, f32[2,4,256,256]{3,2,1,0:T(8,128)S(1)} %copy-done.16, f32[2,4,32,256]{3,2,1,0:T(8,128)S(1)} %copy-done.22, ...), kind=kOutput, calls=%fused_computation.4 | convolution fusion | flops 2331312128 | bytes 29687808 | tf_op jit(solution)/shard_map/bcqhp,bcshp->bchqs/dot_general | solution.py:173
  512.0 3.5 fusion.46
  515.5 2.4 add_convert_fusion
  518.0 3.9 multiply_reduce_fusion.14
  521.9 3.8 convolution_bitcast_fusion
  525.7 16.4 %fusion.79 = f32[2048,1024]{0,1:T(8,128)} fusion(bf16[2048,1024]{1,0:T(8,128)(2,1)} %param.23, f32[2048,2048]{0,1:T(8,128)} %get-tuple-element.68, f32[2048]{0:T(1024)S(1)} %copy-done.48, f32[2048]{0:T(1024)S(1)} %copy-done.51), kind=kOutput, calls=%fused_computation.169 | convolution fusion | flops 8602517504 | bytes 29376512 | tf_op jit(solution)/shard_map/ti,td->id/dot_general | solution.py:131
  542.2 13.4 %multiply_reduce_fusion.5 = (f32[2,4,256,128]{2,3,1,0:T(8,128)}, f32[2,4,32,256]{3,2,1,0:T(8,128)S(1)}) fusion(f32[2,4,32,256]{3,2,1,0:T(8,128)S(1)} %copy-done.26, f32[2,4,256,128]{2,3,1,0:T(8,128)} %copy.370, f32[2,4,256,32,64]{2,1,4,3,0:T(4,128)} %reshape.203, bf16[2,1,32,128,64]{3,4,2,0,1:T(8,128)(2,1)S(1)} %copy-done.15, ...), kind=kOutput, calls=%fused_computation.8 | convolution fusion | flops 1113260032 | bytes 23592960 | tf_op jit(solution)/shard_map/bcshp,bchnp->bchsn/dot_general | solution.py:203
  555.6 1.4 copy.393
  559.6 1.4 copy.396
  561.0 4.2 multiply_reduce_fusion.15
  566.4 2.4 rev.7
  568.9 2.2 copy.404
  571.1 8.4 reduce-window.16
  582.4 2.4 copy.424
  584.8 2.3 copy.394
  587.0 4.1 fusion.60
  591.2 1.6 copy.409
  593.0 1.7 fusion.82
  595.8 3.0 convolution_add_fusion
  598.7 1.6 copy.391
  600.3 2.5 copy.388
  602.9 2.7 convolution_add_fusion.1
  605.6 1.6 copy.390
  607.2 4.5 fusion.3
  611.8 26.5 %fusion.14 = f32[2,4,256,32,64]{2,4,3,1,0:T(8,128)S(1)} fusion(f32[2,4,32,64,256]{4,3,2,1,0:T(8,128)S(1)} %fusion.3, f32[32]{0:T(128)S(1)} %copy-done.72, f32[2,4,32,256]{3,2,1,0:T(8,128)S(1)} %copy-done.32, f32[2,4,32,256]{3,2,1,0:T(8,128)S(1)} %copy-done.23, f32[2,4,256,256]{3,2,1,0:T(8,128)S(1)} %copy-done.17, pred[256,256]{1,0:T(8,128)(4,1)S(1)} %copy-done.42, ...), kind=kOutput, calls=%fused_computation.41 | convolution fusion | flops 2264924160 | bytes 44630144 | tf_op jit(solution)/shard_map/bchqs,bcqhp->bcshp/dot_general | solution.py:170
  638.3 12.0 %copy.384 = f32[2,4,256,32,64]{2,1,4,3,0:T(4,128)} copy(f32[2,4,256,32,64]{2,4,3,1,0:T(8,128)S(1)} %fusion.14) | data formatting | bytes 33554432 | tf_op jit(solution)/shard_map/add | solution.py:206
  650.3 20.8 %reshape.209 = f32[2,1024,2048]{1,2,0:T(8,128)} reshape(f32[2,4,256,32,64]{2,1,4,3,0:T(4,128)} %copy.384) | data formatting | bytes 33554432 | tf_op jit(solution)/shard_map/reshape | solution.py:225
  671.0 43.9 %fusion.80 = (f32[2304]{0:T(1024)S(1)}, f32[2304]{0:T(1024)S(1)}, f32[2304]{0:T(1024)S(1)}, f32[2304]{0:T(1024)S(1)}, f32[2304]{0:T(1024)S(1)}, /*index=5*/f32[2,1024,2304]{1,2,0:T(8,128)}) fusion(f32[288,2,8,1024]{3,2,1,0:T(8,128)} %bitcast.200, f32[2,1024,2304]{1,2,0:T(8,128)} %bitcast.198, f32[2,1024,2304]{1,2,0:T(8,128)} %get-tuple-element.71, ...), kind=kLoop, calls=%fused_computation.170 | loop fusion | flops 89641728 | bytes 94417920 | tf_op jit(solution)/shard_map/reduce_sum | solution.py:232
  714.9 31.4 %fusion.9 = bf16[2,1024,2304]{1,2,0:T(8,128)(2,1)} fusion(f32[2,1024,2304]{1,2,0:T(8,128)} %get-tuple-element.66, f32[2304]{0:T(1024)S(1)} %copy-done.36, f32[2304]{0:T(1024)S(1)} %copy-done.38, f32[2304]{0:T(1024)S(1)} %copy-done.40, f32[2304]{0:T(1024)S(1)} %copy-done.34), kind=kLoop, calls=%fused_computation.27 | loop fusion | flops 37748736 | bytes 28348416 | tf_op jit(solution)/shard_map/convert.4
  746.4 12.4 %copy.392 = bf16[2,1024,2304]{2,1,0:T(8,128)(2,1)} copy(bf16[2,1024,2304]{1,2,0:T(8,128)(2,1)} %fusion.9) | data formatting | bytes 18874368 | tf_op jit(solution)/shard_map/convert.4
  758.8 12.4 %copy.410 = bf16[2048,2048]{1,0:T(8,128)(2,1)} copy(bf16[2048,2048]{0,1:T(8,128)(2,1)} %get-tuple-element.72) | data formatting | bytes 16777216 | tf_op jit(solution)/shard_map/convert.1
  771.2 29.6 %fusion.39 = f32[1024,4384]{1,0:T(8,128)} fusion(bf16[2048,32]{1,0:T(8,128)(2,1)S(1)} %copy-done.24, bf16[2048,2304]{1,0:T(8,128)(2,1)} %bitcast.208, bf16[2048,2048]{1,0:T(8,128)(2,1)} %copy.410, bf16[2048,1024]{1,0:T(8,128)(2,1)} %param.13, f32[1024]{0:T(1024)S(1)} %copy-done.54, f32[2048]{0:T(1024)S(1)} %copy-done.46), kind=kOutput, calls=%fused_computation.82 | convolution fusion | flops 18450087936 | bytes 40120320 | tf_op jit(solution)/shard_map/td,te->de/dot_general | solution.py:252
  800.9 11.8 %fusion.17 = f32[2048]{0:T(1024)S(1)} fusion(f32[256,2,8,1024]{3,2,1,0:T(8,128)} %bitcast.202, f32[2,1024,2304]{1,2,0:T(8,128)} %get-tuple-element.70), kind=kLoop, calls=%fused_computation.45 | loop fusion | flops 8386560 | bytes 33562624 | tf_op jit(solution)/shard_map/reduce_sum | solution.py:168
  813.0 28.2 %fusion.36 = (f32[1024]{0:T(1024)S(1)}, f32[2048]{0:T(1024)S(1)}, f32[2048,1024]{1,0:T(8,128)}) fusion(bf16[2048,1024]{1,0:T(8,128)(2,1)} %param.13, f32[2048]{0:T(1024)S(1)} %copy-done.46, f32[1024]{0:T(1024)S(1)} %copy-done.54, bf16[1024,4384]{1,0:T(8,128)(2,1)} %all-gather.4.cloned.1.call-done, bf16[2048,32]{1,0:T(8,128)(2,1)S(1)} %copy-done.24, ...), kind=kOutput, calls=%fused_computation.79 | convolution fusion | flops 18456377344 | bytes 39542784 | tf_op jit(solution)/shard_map/te,de->td/dot_general | solution.py:255
  841.2 42.3 %all-reduce.12 = (f32[4,2304]{1,0:T(4,128)S(1)}, f32[2304]{0:T(1024)S(1)}, f32[1024]{0:T(1024)S(1)}, f32[2048]{0:T(1024)S(1)}, f32[32]{0:T(128)S(1)}, /*index=5*/f32[32]{0:T(128)S(1)}, f32[32]{0:T(128)S(1)}) all-reduce(f32[4,2304]{1,0:T(4,128)S(1)} %pad_maximum_fusion.5, ...), channel_id=4, replica_groups=mesh['dp'=8,'fsdp'=4] {'dp','fsdp'}, use_global_device_ids=true, to_apply=%region_26.27.clone | all-reduce | flops 14688 | bytes 117504
  887.7 8.9 fusion.31
  896.6 15.9 %fusion.33 = bf16[2048,1024]{1,0:T(8,128)(2,1)} fusion(bf16[2048,1024]{1,0:T(8,128)(2,1)S(1)} %copy-done.2, bf16[2048,1024]{0,1:T(8,128)(2,1)} %all-gather.6.cloned.1.call-done, f32[2048,2048]{0,1:T(8,128)} %get-tuple-element.68, f32[2048]{0:T(1024)S(1)} %copy-done.49, f32[2048]{0:T(1024)S(1)} %copy-done.52), kind=kOutput, calls=%fused_computation.76 | convolution fusion | flops 8608808960 | bytes 29376512 | tf_op jit(solution)/shard_map/dot_general | solution.py:93
  912.5 86.6 %reduce-scatter.4.cloned.1.call-done = f32[32,4384]{1,0:T(8,128)} async-done(((f32[1024,4384]{1,0:T(8,128)}), f32[32,4384]{1,0:T(8,128)}) %reduce-scatter.4.cloned.1.call-update) | async-done | bytes 561168 | tf_op jit(solution)/shard_map/reduce_scatter | solution.py:328
  (231 shorter events, 30.9 us)
Async XLA Ops:
  7.2 102.1 %all-gather.4.cloned.1.call-start = ((), (), s32[]{:S(2)}) async-start(), calls=%async_computation.2 | async-start | bytes 9461760 | tf_op jit(solution)/shard_map/all_gather | solution.py:290
  7.9 370.5 %all-gather.6.cloned.1.call-start = ((), (), s32[]{:S(2)}) async-start(), calls=%async_computation.3 | async-start | bytes 4325376 | tf_op jit(solution)/shard_map/all_gather | solution.py:291
  8.7 903.9 %reduce-scatter.6.cloned.1.call-start = ((), (), s32[]{:S(2)}) async-start(), calls=%async_computation.5 | async-start | bytes 8650752 | tf_op jit(solution)/shard_map/reduce_scatter | solution.py:329
  8.7 452.6 %copy-start.41 = (pred[256,256]{1,0:T(8,128)(4,1)}, pred[256,256]{1,0:T(8,128)(4,1)S(1)}, u32[]{:S(2)}) copy-start(pred[256,256]{1,0:T(8,128)(4,1)S(1)} %iota_compare_fusion) | copy-start | bytes 196612
  54.6 82.3 %copy-start.53 = (f32[1024]{0:T(1024)}, f32[1024]{0:T(1024)S(1)}, u32[]{:S(2)}) copy-start(f32[1024]{0:T(1024)S(1)} %convert_element_type.94) | copy-start | bytes 12292
  57.7 79.2 %copy-start.45 = (f32[2048]{0:T(1024)}, f32[2048]{0:T(1024)S(1)}, u32[]{:S(2)}) copy-start(f32[2048]{0:T(1024)S(1)} %add_rsqrt_fusion.1) | copy-start | bytes 24580
  98.0 78.2 %copy-start.33 = (f32[2304]{0:T(1024)}, f32[2304]{0:T(1024)S(1)}, u32[]{:S(2)}) copy-start(f32[2304]{0:T(1024)S(1)} %get-tuple-element.45) | copy-start | bytes 27652
  98.0 78.2 %copy-start.35 = (f32[2304]{0:T(1024)}, f32[2304]{0:T(1024)S(1)}, u32[]{:S(2)}) copy-start(f32[2304]{0:T(1024)S(1)} %get-tuple-element.46) | copy-start | bytes 27652
  98.0 78.2 %copy-start.37 = (f32[2304]{0:T(1024)}, f32[2304]{0:T(1024)S(1)}, u32[]{:S(2)}) copy-start(f32[2304]{0:T(1024)S(1)} %get-tuple-element.47) | copy-start | bytes 27652
  98.0 78.2 %copy-start.39 = (f32[2304]{0:T(1024)}, f32[2304]{0:T(1024)S(1)}, u32[]{:S(2)}) copy-start(f32[2304]{0:T(1024)S(1)} %get-tuple-element.48) | copy-start | bytes 27652
  108.6 28.3 %copy-start.69 = (f32[32]{0:T(128)}, f32[32]{0:T(128)S(1)}, u32[]{:S(2)}) copy-start(f32[32]{0:T(128)S(1)} %get-tuple-element.57) | copy-start | bytes 388
  108.6 43.6 %copy-start.63 = (f32[32]{0:T(128)}, f32[32]{0:T(128)S(1)}, u32[]{:S(2)}) copy-start(f32[32]{0:T(128)S(1)} %get-tuple-element.56) | copy-start | bytes 388
  108.6 175.1 %copy-start.71 = (f32[32]{0:T(128)}, f32[32]{0:T(128)S(1)}, u32[]{:S(2)}) copy-start(f32[32]{0:T(128)S(1)} %get-tuple-element.58) | copy-start | bytes 388
  108.6 45.3 %copy-start.65 = (f32[32]{0:T(128)}, f32[32]{0:T(128)S(1)}, u32[]{:S(2)}) copy-start(f32[32]{0:T(128)S(1)} %exponential_negate_fusion) | copy-start | bytes 388
  154.0 103.7 %copy-start.5 = (f32[2,4,256,32]{3,1,2,0:T(4,128)}, f32[2,4,256,32]{3,1,2,0:T(4,128)S(1)}, u32[]{:S(2)}) copy-start(f32[2,4,256,32]{3,1,2,0:T(4,128)S(1)} %copy.361) | copy-start | bytes 786436
  159.6 16.6 %copy-start.20 = (f32[2,4,32,256]{3,2,1,0:T(8,128)}, f32[2,4,32,256]{3,2,1,0:T(8,128)S(1)}, u32[]{:S(2)}) copy-start(f32[2,4,32,256]{3,2,1,0:T(8,128)S(1)} %copy_bitcast_fusion.1) | copy-start | bytes 786436
  160.0 97.7 %copy-start.9 = (f32[2,4,32,256]{2,1,3,0:T(4,128)}, f32[2,4,32,256]{2,1,3,0:T(4,128)S(1)}, u32[]{:S(2)}) copy-start(f32[2,4,32,256]{2,1,3,0:T(4,128)S(1)} %copy.367) | copy-start | bytes 786436
  160.0 97.7 %copy-start.43 = (f32[2,4,32]{2,1,0:T(4,128)}, f32[2,4,32]{2,1,0:T(4,128)S(1)}, u32[]{:S(2)}) copy-start(f32[2,4,32]{2,1,0:T(4,128)S(1)} %slice_bitcast_fusion) | copy-start | bytes 3076
  255.0 26.6 %copy-start.7 = (bf16[2,1024,128]{2,1,0:T(8,128)(2,1)}, bf16[2,1024,128]{2,1,0:T(8,128)(2,1)S(1)}, u32[]{:S(2)}) copy-start(bf16[2,1024,128]{2,1,0:T(8,128)(2,1)S(1)} %copy.359) | copy-start | bytes 1572868
  256.5 25.1 %copy-start.11 = (bf16[2,1024,128]{2,1,0:T(8,128)(2,1)}, bf16[2,1024,128]{2,1,0:T(8,128)(2,1)S(1)}, u32[]{:S(2)}) copy-start(bf16[2,1024,128]{2,1,0:T(8,128)(2,1)S(1)} %copy.360) | copy-start | bytes 1572868
  260.6 16.6 %copy-start.25 = (f32[2,4,32,256]{3,2,1,0:T(8,128)}, f32[2,4,32,256]{3,2,1,0:T(8,128)S(1)}, u32[]{:S(2)}) copy-start(f32[2,4,32,256]{3,2,1,0:T(8,128)S(1)} %copy.369) | copy-start | bytes 786436
  261.2 16.0 %copy-start.55 = (f32[2,1,32]{2,1,0:T(1,128)}, f32[2,1,32]{2,1,0:T(1,128)S(1)}, u32[]{:S(2)}) copy-start(f32[2,1,32]{2,1,0:T(1,128)S(1)} %get-tuple-element.88) | copy-start | bytes 772
  261.2 16.0 %copy-start.57 = (f32[2,1,32]{2,1,0:T(1,128)}, f32[2,1,32]{2,1,0:T(1,128)S(1)}, u32[]{:S(2)}) copy-start(f32[2,1,32]{2,1,0:T(1,128)S(1)} %get-tuple-element.89) | copy-start | bytes 772
  261.2 16.0 %copy-start.60 = (f32[2,1,32]{2,1,0:T(1,128)}, f32[2,1,32]{2,1,0:T(1,128)S(1)}, u32[]{:S(2)}) copy-start(f32[2,1,32]{2,1,0:T(1,128)S(1)} %get-tuple-element.90) | copy-start | bytes 772
  281.7 37.8 %copy-start = (f32[2,4,256,2048]{2,3,1,0}, f32[2,4,256,2048]{2,3,1,0:S(1)}, u32[]{:S(2)}) copy-start(f32[2,4,256,2048]{2,3,1,0:S(1)} %fusion.92) | copy-start | bytes 50331652
  361.1 17.3 %copy-start.47 = (f32[2048]{0:T(1024)S(1)}, f32[2048]{0:T(1024)}, u32[]{:S(2)}) copy-start(f32[2048]{0:T(1024)} %convert_element_type.102) | copy-start | bytes 24580
  378.4 21.0 %copy-start.50 = (f32[2048]{0:T(1024)}, f32[2048]{0:T(1024)S(1)}, u32[]{:S(2)}) copy-start(f32[2048]{0:T(1024)S(1)} %add_rsqrt_fusion) | copy-start | bytes 24580
  449.0 12.4 %copy-start.1 = (bf16[2,4,256,32,64]{2,1,0,4,3:T(4,128)(2,1)S(1)}, bf16[2,4,256,32,64]{2,1,0,4,3:T(4,128)(2,1)}, u32[]{:S(2)}) copy-start(bf16[2,4,256,32,64]{2,1,0,4,3:T(4,128)(2,1)} %reshape.208) | copy-start | bytes 25165828
  449.0 12.4 %copy-start.16 = (f32[2,4,256,256]{3,2,1,0:T(8,128)S(1)}, f32[2,4,256,256]{3,2,1,0:T(8,128)}, u32[]{:S(2)}) copy-start(f32[2,4,256,256]{3,2,1,0:T(8,128)} %fusion.91) | copy-start | bytes 6291460
  449.0 12.4 %copy-start.22 = (f32[2,4,32,256]{3,2,1,0:T(8,128)S(1)}, f32[2,4,32,256]{3,2,1,0:T(8,128)}, u32[]{:S(2)}) copy-start(f32[2,4,32,256]{3,2,1,0:T(8,128)} %copy-done.20) | copy-start | bytes 786436
  449.0 12.4 %copy-start.31 = (f32[2,4,32,256]{3,2,1,0:T(8,128)S(1)}, f32[2,4,32,256]{3,2,1,0:T(8,128)}, u32[]{:S(2)}) copy-start(f32[2,4,32,256]{3,2,1,0:T(8,128)} %copy-done.30) | copy-start | bytes 786436
  512.0 9.9 copy-start.4
  525.7 16.5 %copy-start.15 = (bf16[2,1,32,128,64]{3,4,2,0,1:T(8,128)(2,1)S(1)}, bf16[2,1,32,128,64]{3,4,2,0,1:T(8,128)(2,1)}, u32[]{:S(2)}) copy-start(bf16[2,1,32,128,64]{3,4,2,0,1:T(8,128)(2,1)} %copy-done.14) | copy-start | bytes 3145732
  525.7 16.5 %copy-start.26 = (f32[2,4,32,256]{3,2,1,0:T(8,128)S(1)}, f32[2,4,32,256]{3,2,1,0:T(8,128)}, u32[]{:S(2)}) copy-start(f32[2,4,32,256]{3,2,1,0:T(8,128)} %copy-done.25) | copy-start | bytes 786436
  542.2 14.8 %copy-start.18 = (f32[2,4,256,32]{2,3,1,0:T(8,128)S(1)}, f32[2,4,256,32]{2,3,1,0:T(8,128)}, u32[]{:S(2)}) copy-start(f32[2,4,256,32]{2,3,1,0:T(8,128)} %get-tuple-element.75) | copy-start | bytes 786436
  542.2 16.1 %copy-start.29 = (f32[2,4,32,256]{3,2,1,0:T(8,128)S(1)}, f32[2,4,32,256]{3,2,1,0:T(8,128)}, u32[]{:S(2)}) copy-start(f32[2,4,32,256]{3,2,1,0:T(8,128)} %get-tuple-element.24) | copy-start | bytes 786436
  542.2 17.4 %copy-start.28 = (f32[2,4,32,256]{3,2,1,0:T(8,128)S(1)}, f32[2,4,32,256]{3,2,1,0:T(8,128)}, u32[]{:S(2)}) copy-start(f32[2,4,32,256]{3,2,1,0:T(8,128)} %get-tuple-element.23) | copy-start | bytes 786436
  542.2 23.0 %copy-start.10 = (f32[2,4,32,256]{2,1,3,0:T(4,128)S(1)}, f32[2,4,32,256]{2,1,3,0:T(4,128)}, u32[]{:S(2)}) copy-start(f32[2,4,32,256]{2,1,3,0:T(4,128)} %copy-done.9) | copy-start | bytes 786436
  555.6 31.4 %copy-start.6 = (f32[2,4,256,32]{3,1,2,0:T(4,128)S(1)}, f32[2,4,256,32]{3,1,2,0:T(4,128)}, u32[]{:S(2)}) copy-start(f32[2,4,256,32]{3,1,2,0:T(4,128)} %copy-done.5) | copy-start | bytes 786436
  555.6 31.4 %copy-start.44 = (f32[2,4,32]{2,1,0:T(4,128)S(1)}, f32[2,4,32]{2,1,0:T(4,128)}, u32[]{:S(2)}) copy-start(f32[2,4,32]{2,1,0:T(4,128)} %copy-done.43) | copy-start | bytes 3076
  555.6 31.4 %copy-start.66 = (f32[32]{0:T(128)S(1)}, f32[32]{0:T(128)}, u32[]{:S(2)}) copy-start(f32[32]{0:T(128)} %copy-done.65) | copy-start | bytes 388
  555.6 37.3 %copy-start.64 = (f32[32]{0:T(128)S(1)}, f32[32]{0:T(128)}, u32[]{:S(2)}) copy-start(f32[32]{0:T(128)} %copy-done.63) | copy-start | bytes 388
  559.6 36.2 %copy-start.12 = (bf16[2,1024,128]{2,1,0:T(8,128)(2,1)S(1)}, bf16[2,1024,128]{2,1,0:T(8,128)(2,1)}, u32[]{:S(2)}) copy-start(bf16[2,1024,128]{2,1,0:T(8,128)(2,1)} %copy-done.11) | copy-start | bytes 1572868
  566.4 36.4 %copy-start.8 = (bf16[2,1024,128]{2,1,0:T(8,128)(2,1)S(1)}, bf16[2,1024,128]{2,1,0:T(8,128)(2,1)}, u32[]{:S(2)}) copy-start(bf16[2,1024,128]{2,1,0:T(8,128)(2,1)} %copy-done.7) | copy-start | bytes 1572868
  582.4 24.8 %copy-start.27 = (f32[2,4,32,256]{3,2,1,0:T(8,128)S(1)}, f32[2,4,32,256]{3,2,1,0:T(8,128)}, u32[]{:S(2)}) copy-start(f32[2,4,32,256]{3,2,1,0:T(8,128)} %copy-done.25) | copy-start | bytes 786436
  591.2 11.7 %copy-start.13 = (bf16[2,4,256,256]{3,2,1,0:T(8,128)(2,1)S(1)}, bf16[2,4,256,256]{3,2,1,0:T(8,128)(2,1)}, u32[]{:S(2)}) copy-start(bf16[2,4,256,256]{3,2,1,0:T(8,128)(2,1)} %get-tuple-element.26) | copy-start | bytes 3145732
  595.7 403.5 %reduce-scatter.4.cloned.1.call-start = ((), (), s32[]{:S(2)}) async-start(), calls=%async_computation.4 | async-start | bytes 18923520 | tf_op jit(solution)/shard_map/reduce_scatter | solution.py:328
  602.9 8.9 copy-start.32
  602.9 8.9 copy-start.42
  602.9 8.9 copy-start.72
  671.0 43.9 %copy-start.34 = (f32[2304]{0:T(1024)S(1)}, f32[2304]{0:T(1024)}, u32[]{:S(2)}) copy-start(f32[2304]{0:T(1024)} %copy-done.33) | copy-start | bytes 27652
  671.0 43.9 %copy-start.36 = (f32[2304]{0:T(1024)S(1)}, f32[2304]{0:T(1024)}, u32[]{:S(2)}) copy-start(f32[2304]{0:T(1024)} %copy-done.35) | copy-start | bytes 27652
  671.0 43.9 %copy-start.38 = (f32[2304]{0:T(1024)S(1)}, f32[2304]{0:T(1024)}, u32[]{:S(2)}) copy-start(f32[2304]{0:T(1024)} %copy-done.37) | copy-start | bytes 27652
  671.0 43.9 %copy-start.40 = (f32[2304]{0:T(1024)S(1)}, f32[2304]{0:T(1024)}, u32[]{:S(2)}) copy-start(f32[2304]{0:T(1024)} %copy-done.39) | copy-start | bytes 27652
  746.4 24.8 %copy-start.24 = (bf16[2048,32]{1,0:T(8,128)(2,1)S(1)}, bf16[2048,32]{1,0:T(8,128)(2,1)}, u32[]{:S(2)}) copy-start(bf16[2048,32]{1,0:T(8,128)(2,1)} %copy.411) | copy-start | bytes 393220
  746.4 24.8 %copy-start.46 = (f32[2048]{0:T(1024)S(1)}, f32[2048]{0:T(1024)}, u32[]{:S(2)}) copy-start(f32[2048]{0:T(1024)} %copy-done.45) | copy-start | bytes 24580
  746.4 24.8 %copy-start.54 = (f32[1024]{0:T(1024)S(1)}, f32[1024]{0:T(1024)}, u32[]{:S(2)}) copy-start(f32[1024]{0:T(1024)} %copy-done.53) | copy-start | bytes 12292
  800.9 12.0 %copy-start.68 = (f32[32]{0:T(128)S(1)}, f32[32]{0:T(128)}, u32[]{:S(2)}) copy-start(f32[32]{0:T(128)} %get-tuple-element.85) | copy-start | bytes 388
  800.9 12.0 %copy-start.70 = (f32[32]{0:T(128)S(1)}, f32[32]{0:T(128)}, u32[]{:S(2)}) copy-start(f32[32]{0:T(128)} %copy-done.69) | copy-start | bytes 388
  812.9 28.2 %copy-start.62 = (f32[2048]{0:T(1024)S(1)}, f32[2048]{0:T(1024)}, u32[]{:S(2)}) copy-start(f32[2048]{0:T(1024)} %get-tuple-element.30) | copy-start | bytes 24580
  812.9 28.2 %copy-start.67 = (f32[32]{0:T(128)S(1)}, f32[32]{0:T(128)}, u32[]{:S(2)}) copy-start(f32[32]{0:T(128)} %get-tuple-element.64) | copy-start | bytes 388
  841.1 55.5 %copy-start.49 = (f32[2048]{0:T(1024)S(1)}, f32[2048]{0:T(1024)}, u32[]{:S(2)}) copy-start(f32[2048]{0:T(1024)} %convert_element_type.102) | copy-start | bytes 24580
  841.1 55.5 %copy-start.52 = (f32[2048]{0:T(1024)S(1)}, f32[2048]{0:T(1024)}, u32[]{:S(2)}) copy-start(f32[2048]{0:T(1024)} %copy-done.50) | copy-start | bytes 24580
  883.5 13.1 %copy-start.2 = (bf16[2048,1024]{1,0:T(8,128)(2,1)S(1)}, bf16[2048,1024]{1,0:T(8,128)(2,1)}, u32[]{:S(2)}) copy-start(bf16[2048,1024]{1,0:T(8,128)(2,1)} %param.13) | copy-start | bytes 12582916
  (13 other events, 66.7 us)
Sparse Core Ops, SparseCore 0:
  10.9 84.0 all-gather.3
  97.8 60.6 all-gather.5
  595.8 146.2 reduce-scatter.5
  800.9 198.1 reduce-scatter.3
where the time goes:
time: 1010 us
  matrix products  299 us (30%)
  other arithmetic  249 us (25%)
  local copies, waits for them, and re-layouts  222 us (22%)
  blocking collectives  132 us (13%)
  waiting for transfers between devices  88 us (9%)
  between operations  15.6 us (2%)
    another operation x10, other arithmetic  95.3 us
    unnamed x3, blocking collectives  91.7 us
    reduce_scatter x1, waiting for transfers between devices, on_device(): lax.psum_scatter(in_weight_grad, ('dp', 'fsdp'), scatter_dimension=0, til...  86.6 us
    dot_general x1, matrix products, mixer_side(): jnp.einsum('bcqhp,bcshp->bchqs', ssm_grad, values_low, preferred_element_...  50.6 us
    reduce_sum x1, other arithmetic, mixer_side(): conv_bias_grad = jnp.sum(pre_grad, axis=(0, 1))  43.9 us
    all_gather x1, blocking collectives, on_device(): lax.all_gather(conv_weight, ('dp', 'fsdp'), axis=1, tiled=True)  40.1 us
    dot_general x1, matrix products, forward_pass(): jnp.einsum('bchqs,bcshp->bcqhp', mixing, values_low, preferred_element_ty...  35.8 us
    convert_element_type x1, other arithmetic, mixer_side(): values_grad = skip_scale[:, None] * ssm_grad  35.1 us
  transfers between devices with their start and end apart: 4, of which 1 were waited for; matrix products, arithmetic and copies ran while one was open for 55% of the time, Pallas kernels for 0%

commit v1 on v0

v1 whole, which is shorter than its diff:
```python
import jax
import jax.numpy as jnp
from jax import lax
from jax.experimental import pallas as pl
from jax.experimental.pallas import tpu as pltpu
from jax.sharding import PartitionSpec as P

HEADS = 32
HEADDIM = 64
STATE = 128
KCONV = 4
GROUP = 256
SEQ_LEN = 1024
GROUPS = SEQ_LEN // GROUP
INNER = 2048
CONVDIM = 2304
PAIR = 2 * HEADDIM
EPSILON = 1e-05
AXES = ("dp", "fsdp")
f32 = jnp.float32
bf16 = jnp.bfloat16


def silu_slope(pre_act):
    logistic = jax.nn.sigmoid(pre_act)
    return logistic * (1.0 + pre_act * (1.0 - logistic))


def mm(a, b):
    return lax.dot_general(a, b, (((1,), (0,)), ((), ())), preferred_element_type=f32)


def mm_nt(a, b):
    return lax.dot_general(a, b, (((1,), (1,)), ((), ())), preferred_element_type=f32)


def mm_tn(a, b):
    return lax.dot_general(a, b, (((0,), (0,)), ((), ())), preferred_element_type=f32)


def causal_mask():
    rows = lax.broadcasted_iota(jnp.int32, (GROUP, GROUP), 0)
    return rows >= lax.broadcasted_iota(jnp.int32, (GROUP, GROUP), 1)


def scan_kernel(act_ref, cum_ref, step_ref, cum_t_ref, step_t_ref, skip_ref, y_ref, ent_ref, state):
    @pl.when(pl.program_id(0) % GROUPS == 0)
    def _():
        state[...] = jnp.zeros_like(state)

    b_low = act_ref[:, INNER : INNER + STATE]
    c_low = act_ref[:, INNER + STATE :]
    gram = jnp.where(causal_mask(), mm_nt(c_low, b_low), 0.0)
    cum = cum_ref[...]
    last = cum_ref[GROUP - 1 : GROUP, :]
    growth = jnp.exp(cum)
    weight = jnp.exp(last - cum) * step_ref[...]
    decay = jnp.exp(last)
    first = lax.broadcasted_iota(jnp.int32, (GROUP, PAIR), 1) < HEADDIM
    for pair in range(HEADS // 2):
        at = slice(pair * PAIR, (pair + 1) * PAIR)
        vals = act_ref[:, at]
        low, high = 2 * pair, 2 * pair + 1
        parts = []
        for head in (low, high):
            differ = cum[:, head : head + 1] - cum_t_ref[0, head : head + 1, :]
            table = jnp.exp(jnp.minimum(differ, 0.0))
            mixing = (gram * table * step_t_ref[0, head : head + 1, :]).astype(bf16)
            parts.append(mm(mixing, vals))

        def spread(cols):
            lanes = first[: cols.shape[0]]
            return jnp.where(lanes, cols[:, low : low + 1], cols[:, high : high + 1])

        carried = state[:, at]
        ent = carried.astype(bf16)
        ent_ref[0, :, at] = ent
        wide = vals.astype(f32)
        y_ref[:, at] = (
            jnp.where(first, parts[0], parts[1])
            + spread(growth) * mm(c_low, ent)
            + skip_ref[:, at] * wide
        )
        weighted = (spread(weight) * wide).astype(bf16)
        state[:, at] = spread(decay) * carried + mm_tn(b_low, weighted)


def scan_back_kernel(
    dy_ref, act_ref, ent_ref, cum_ref, step_ref, cum_t_ref, step_t_ref, skip_ref,
    dact_ref, row_ref, wg_ref, col_ref, stat_ref, carried_ref, gram_acc, b_acc, c_acc,
):
    @pl.when(pl.program_id(0) % GROUPS == 0)
    def _():
        carried_ref[...] = jnp.zeros_like(carried_ref)

    b_low = act_ref[:, INNER : INNER + STATE]
    c_low = act_ref[:, INNER + STATE :]
    causal = causal_mask()
    gram = jnp.where(causal, mm_nt(c_low, b_low), 0.0)
    gram_acc[...] = jnp.zeros_like(gram_acc)
    b_acc[...] = jnp.zeros_like(b_acc)
    c_acc[...] = jnp.zeros_like(c_acc)
    cum = cum_ref[...]
    last = cum_ref[GROUP - 1 : GROUP, :]
    growth = jnp.exp(cum)
    weight = jnp.exp(last - cum) * step_ref[...]
    decay = jnp.exp(last)
    first = lax.broadcasted_iota(jnp.int32, (GROUP, PAIR), 1) < HEADDIM
    for pair in range(HEADS // 2):
        at = slice(pair * PAIR, (pair + 1) * PAIR)
        vals = act_ref[:, at]
        dy = dy_ref[:, at]
        low, high = 2 * pair, 2 * pair + 1
        wide = vals.astype(f32)
        dy_wide = dy.astype(f32)
        parts = []
        row_sums = []
        for head in (low, high):
            differ = cum[:, head : head + 1] - cum_t_ref[0, head : head + 1, :]
            table = jnp.exp(jnp.minimum(differ, 0.0))
            steps = step_t_ref[0, head : head + 1, :]
            own = first if head == low else jnp.logical_not(first)
            mixing_grad = mm_nt(jnp.where(own, dy_wide, 0.0).astype(bf16), vals)
            shaded = gram * table
            mixing = shaded * steps
            col_ref[0, head : head + 1, :] = jnp.sum(mixing_grad * shaded, axis=0, keepdims=True)
            row_sums.append(jnp.sum(mixing_grad * mixing, axis=1, keepdims=True))
            gram_acc[...] += mixing_grad * (table * steps)
            parts.append(mm_tn(mixing.astype(bf16), dy))

        def spread(cols):
            lanes = first[: cols.shape[0]]
            return jnp.where(lanes, cols[:, low : low + 1], cols[:, high : high + 1])

        ent = ent_ref[0, :, at]
        carried = carried_ref[:, at]
        state_grad = carried.astype(bf16)
        from_state = mm(b_low, state_grad)
        weights = spread(weight)
        dact_ref[:, at] = (
            jnp.where(first, parts[0], parts[1]) + weights * from_state + skip_ref[:, at] * dy_wide
        )
        raw = spread(growth) * dy_wide
        raw_low = raw.astype(bf16)
        inter = raw * mm(c_low, ent)
        state_term = wide * from_state
        for head, sums, own in ((low, row_sums[0], first), (high, row_sums[1], jnp.logical_not(first))):
            row_ref[:, head : head + 1] = sums + jnp.sum(
                jnp.where(own, inter, 0.0), axis=1, keepdims=True
            )
            wg_ref[:, head : head + 1] = jnp.sum(
                jnp.where(own, state_term, 0.0), axis=1, keepdims=True
            )
        stat_ref[0, 0:1, at] = jnp.sum(carried * ent.astype(f32), axis=0, keepdims=True)
        stat_ref[0, 1:2, at] = jnp.sum(dy_wide * wide, axis=0, keepdims=True)
        carried_ref[:, at] = mm_tn(c_low, raw_low) + spread(decay) * carried
        c_acc[...] += mm_nt(raw_low, ent)
        b_acc[...] += mm_nt((weights * wide).astype(bf16), state_grad)
    stat_ref[0, 2:8, :] = jnp.zeros((6, INNER), f32)
    gram_grad = jnp.where(causal, gram_acc[...], 0.0).astype(bf16)
    dact_ref[:, INNER : INNER + STATE] = b_acc[...] + mm_tn(gram_grad, c_low)
    dact_ref[:, INNER + STATE :] = c_acc[...] + mm(gram_grad, b_low)


def specs_for(order):
    def rows(width):
        return pl.BlockSpec((GROUP, width), lambda g: (order(g), 0))

    def cube(height, width):
        return pl.BlockSpec((1, height, width), lambda g: (order(g), 0, 0))

    return rows, cube, pl.BlockSpec((1, INNER), lambda g: (0, 0))


def scan_forward(act, cum, step, cum_t, step_t, skip):
    count = act.shape[0] // GROUP
    rows, cube, whole = specs_for(lambda g: g)
    return pl.pallas_call(
        scan_kernel,
        grid=(count,),
        in_specs=[rows(CONVDIM), rows(HEADS), rows(HEADS), cube(HEADS, GROUP), cube(HEADS, GROUP), whole],
        out_specs=[rows(INNER), cube(STATE, INNER)],
        out_shape=[
            jax.ShapeDtypeStruct((act.shape[0], INNER), f32),
            jax.ShapeDtypeStruct((count, STATE, INNER), bf16),
        ],
        scratch_shapes=[pltpu.VMEM((STATE, INNER), f32)],
        compiler_params=pltpu.CompilerParams(
            dimension_semantics=("arbitrary",), vmem_limit_bytes=40 * 2**20
        ),
        cost_estimate=pl.CostEstimate(
            flops=count * 2 * 10**9, bytes_accessed=act.shape[0] * 15000, transcendentals=count * 2**21
        ),
    )(act, cum, step, cum_t, step_t, skip)


def scan_backward(dy, act, ent, cum, step, cum_t, step_t, skip):
    count = act.shape[0] // GROUP
    rows, cube, whole = specs_for(lambda g: g // GROUPS * GROUPS + GROUPS - 1 - g % GROUPS)
    return pl.pallas_call(
        scan_back_kernel,
        grid=(count,),
        in_specs=[
            rows(INNER), rows(CONVDIM), cube(STATE, INNER), rows(HEADS), rows(HEADS),
            cube(HEADS, GROUP), cube(HEADS, GROUP), whole,
        ],
        out_specs=[rows(CONVDIM), rows(HEADS), rows(HEADS), cube(HEADS, GROUP), cube(8, INNER)],
        out_shape=[
            jax.ShapeDtypeStruct((act.shape[0], CONVDIM), f32),
            jax.ShapeDtypeStruct((act.shape[0], HEADS), f32),
            jax.ShapeDtypeStruct((act.shape[0], HEADS), f32),
            jax.ShapeDtypeStruct((count, HEADS, GROUP), f32),
            jax.ShapeDtypeStruct((count, 8, INNER), f32),
        ],
        scratch_shapes=[
            pltpu.VMEM((STATE, INNER), f32),
            pltpu.VMEM((GROUP, GROUP), f32),
            pltpu.VMEM((GROUP, STATE), f32),
            pltpu.VMEM((GROUP, STATE), f32),
        ],
        compiler_params=pltpu.CompilerParams(
            dimension_semantics=("arbitrary",), vmem_limit_bytes=40 * 2**20
        ),
        cost_estimate=pl.CostEstimate(
            flops=count * 4 * 10**9, bytes_accessed=act.shape[0] * 20000, transcendentals=count * 2**21
        ),
    )(dy, act, ent, cum, step, cum_t, step_t, skip)


def group_cumsum(a, suffix):
    tri = causal_mask().astype(f32)
    return jnp.einsum(
        "rt,grh->gth" if suffix else "tr,grh->gth",
        tri, a.reshape(-1, GROUP, HEADS), precision=lax.Precision.HIGHEST,
    ).reshape(-1, HEADS)


def gather_weights(in_weight, conv_weight, conv_bias, norm_gain, gate_gain):
    rows, cols = in_weight.shape
    spare = -cols % 128
    small = jnp.concatenate([conv_weight.reshape(-1), conv_bias, norm_gain, gate_gain])
    side = jnp.pad(small, (0, rows * spare - small.shape[0])).reshape(rows, spare)
    whole = lax.all_gather(
        jnp.concatenate([in_weight, side], axis=1), AXES, axis=0, tiled=True
    )
    side = whole[:, cols:].reshape(-1, rows * spare)
    devices = side.shape[0]
    start = 0
    pieces = []
    for size in (conv_weight.size, conv_bias.size, norm_gain.size, gate_gain.size):
        pieces.append(side[:, start : start + size])
        start += size
    taps = pieces[0].reshape(devices, KCONV, -1).swapaxes(0, 1).reshape(KCONV, -1)
    return whole, taps, pieces[1].reshape(-1), pieces[2].reshape(-1), pieces[3].reshape(-1)


def on_device(
    tokens, in_weight, out_weight, conv_weight, conv_bias, norm_gain, gate_gain,
    decay_log, step_bias, skip_scale, cotangent,
):
    whole, taps, bias_all, norm_all, gate_all = gather_weights(
        in_weight, conv_weight, conv_bias, norm_gain, gate_gain
    )
    out_all = lax.all_gather(out_weight, AXES, axis=1, tiled=True)
    head_all = lax.all_gather(
        jnp.stack([decay_log, step_bias, skip_scale]), "fsdp", axis=1, tiled=True
    )
    decay_rate = -jnp.exp(head_all[0])
    skip_row = jnp.repeat(head_all[2], HEADDIM)[None]
    seq_count = tokens.shape[0] // SEQ_LEN
    count = tokens.shape[0] // GROUP
    taps = taps.astype(f32)
    norm_all = norm_all.astype(f32)
    gate_all = gate_all.astype(f32)

    inputs = tokens.astype(f32)
    norm_scale = lax.rsqrt(jnp.mean(inputs * inputs, axis=-1, keepdims=True) + EPSILON)
    normed = (inputs * norm_scale * norm_all).astype(bf16)
    w_gate = whole[:, :INNER]
    w_conv = whole[:, INNER : INNER + CONVDIM]
    w_step = whole[:, INNER + CONVDIM : INNER + CONVDIM + HEADS]
    conv_in = mm(normed, w_conv).reshape(seq_count, SEQ_LEN, CONVDIM)
    step_raw = mm(normed, w_step)
    gate_in = mm(normed, w_gate)
    padded = jnp.pad(conv_in, ((0, 0), (KCONV - 1, 0), (0, 0)))
    pre_act = bias_all.astype(f32) + sum(taps[k] * padded[:, k : k + SEQ_LEN] for k in range(KCONV))
    act = jax.nn.silu(pre_act).astype(bf16).reshape(-1, CONVDIM)
    step = jax.nn.softplus(step_raw + head_all[1])
    cum = group_cumsum(step * decay_rate, False)
    cum_t = cum.reshape(count, GROUP, HEADS).swapaxes(1, 2)
    step_t = step.reshape(count, GROUP, HEADS).swapaxes(1, 2)
    ssm_out, ent = scan_forward(act, cum, step, cum_t, step_t, skip_row)

    silu_gate = jax.nn.silu(gate_in)
    gated_out = ssm_out * silu_gate
    gate_scale = lax.rsqrt(jnp.mean(gated_out * gated_out, axis=-1, keepdims=True) + EPSILON)
    mixed_low = (gated_out * gate_scale * gate_all).astype(bf16)
    output = (inputs + mm(mixed_low, out_all)).astype(bf16)

    out_share = lax.psum_scatter(
        mm_tn(mixed_low, cotangent).astype(bf16), AXES, scatter_dimension=1, tiled=True
    ).astype(f32)
    mixed_grad = mm_nt(cotangent, out_all)
    gate_gain_grad = jnp.sum(mixed_grad * gated_out * gate_scale, axis=0)
    scaled_in = mixed_grad * gate_all
    gated_grad = gate_scale * (
        scaled_in
        - gated_out * gate_scale * gate_scale
        * jnp.mean(scaled_in * gated_out, axis=-1, keepdims=True)
    )
    ssm_grad = (gated_grad * silu_gate).astype(bf16)
    gate_grad = (gated_grad * ssm_out * silu_slope(gate_in)).astype(bf16)
    gate_cols = lax.psum_scatter(
        mm_tn(normed, gate_grad).astype(bf16), AXES, scatter_dimension=0, tiled=True
    )

    dact, row, weight_grad, col_t, stats = scan_backward(
        ssm_grad, act, ent, cum, step, cum_t, step_t, skip_row
    )
    col = col_t.swapaxes(1, 2).reshape(-1, HEADS)
    grouped = (count, GROUP, HEADS)
    last = cum.reshape(grouped)[:, -1:]
    fading = jnp.exp(last - cum.reshape(grouped)).reshape(-1, HEADS)
    weight_term = weight_grad * fading * step
    decay_grad = jnp.sum(stats[:, 0].reshape(count, HEADS, HEADDIM), axis=-1)
    last_grad = jnp.sum(weight_term.reshape(grouped), axis=1) + decay_grad * jnp.exp(last[:, 0])
    skip_grad = jnp.sum(stats[:, 1].reshape(count, HEADS, HEADDIM), axis=(0, 2))
    cum_grad = row - step * col - weight_term
    rate_grad = (
        group_cumsum(cum_grad, True).reshape(grouped) + last_grad[:, None]
    ).reshape(-1, HEADS)
    step_grad = col + weight_grad * fading + rate_grad * decay_rate
    decay_log_grad = jnp.sum(rate_grad * step, axis=0) * decay_rate
    step_raw_grad = step_grad * jax.nn.sigmoid(step_raw + head_all[1])
    step_bias_grad = jnp.sum(step_raw_grad, axis=0)

    pre_grad = dact.reshape(seq_count, SEQ_LEN, CONVDIM) * silu_slope(pre_act)
    conv_bias_grad = jnp.sum(pre_grad, axis=(0, 1))
    conv_weight_grad = jnp.stack(
        [jnp.sum(pre_grad * padded[:, k : k + SEQ_LEN], axis=(0, 1)) for k in range(KCONV)]
    )
    grad_padded = jnp.pad(pre_grad, ((0, 0), (0, KCONV - 1), (0, 0)))
    conv_in_grad = sum(
        taps[k] * grad_padded[:, KCONV - 1 - k : KCONV - 1 - k + SEQ_LEN] for k in range(KCONV)
    )
    conv_in_grad = conv_in_grad.astype(bf16).reshape(-1, CONVDIM)
    step_low = step_raw_grad.astype(bf16)
    late = jnp.concatenate([mm_tn(normed, conv_in_grad), mm_tn(normed, step_low)], axis=1)
    late_cols = lax.psum_scatter(late.astype(bf16), AXES, scatter_dimension=0, tiled=True)
    in_share = jnp.concatenate([gate_cols, late_cols], axis=1).astype(f32)
    normed_grad = (
        mm_nt(gate_grad, w_gate) + mm_nt(conv_in_grad, w_conv) + mm_nt(step_low, w_step)
    )
    norm_share = jnp.sum(in_share * in_weight.astype(f32), axis=1) / norm_gain.astype(f32)
    scaled_in = normed_grad * norm_all
    token_grad = norm_scale * (
        scaled_in
        - inputs * norm_scale * norm_scale * jnp.mean(scaled_in * inputs, axis=-1, keepdims=True)
    ) + cotangent.astype(f32)

    totals = lax.psum(
        jnp.concatenate(
            [conv_weight_grad.reshape(-1), conv_bias_grad, gate_gain_grad,
             decay_log_grad, step_bias_grad, skip_grad]
        ),
        AXES,
    )
    me = lax.axis_index("dp") * lax.axis_size("fsdp") + lax.axis_index("fsdp")
    conv_total = totals[: KCONV * CONVDIM].reshape(KCONV, CONVDIM)
    start = KCONV * CONVDIM
    width = conv_weight.shape[1]
    conv_weight_share = lax.dynamic_slice_in_dim(conv_total, me * width, width, axis=1)
    conv_bias_share = lax.dynamic_slice_in_dim(totals, start + me * width, width)
    start += CONVDIM
    wide = gate_gain.shape[0]
    gate_share = lax.dynamic_slice_in_dim(totals, start + me * wide, wide)
    start += INNER
    share = decay_log.shape[0]
    own = lax.axis_index("fsdp") * share
    heads = [
        lax.dynamic_slice_in_dim(totals, start + i * HEADS + own, share) for i in range(3)
    ]
    return (
        output, token_grad.astype(bf16), in_share, out_share, conv_weight_share,
        conv_bias_share, norm_share, gate_share, *heads,
    )


def solution(mesh):
    return jax.shard_map(
        on_device,
        mesh=mesh,
        in_specs=(
            P(("dp", "fsdp"), None),
            P(("dp", "fsdp"), None),
            P(None, ("dp", "fsdp")),
            P(None, ("dp", "fsdp")),
            P(("dp", "fsdp")),
            P(("dp", "fsdp")),
            P(("dp", "fsdp")),
            P("fsdp"),
            P("fsdp"),
            P("fsdp"),
            P(("dp", "fsdp"), None),
        ),
        out_specs=(
            P(("dp", "fsdp"), None),
            P(("dp", "fsdp"), None),
            P(("dp", "fsdp"), None),
            P(None, ("dp", "fsdp")),
            P(None, ("dp", "fsdp")),
            P(("dp", "fsdp")),
            P(("dp", "fsdp")),
            P(("dp", "fsdp")),
            P("fsdp"),
            P("fsdp"),
            P("fsdp"),
        ),
        check_vma=False,
    )
```

time: 1010 us -> 742 us (0.73)
  local copies, waits for them, and re-layouts: 222 us -> 20.9 us
  Pallas kernels: 0 us -> 159 us
  matrix products: 299 us -> 161 us
  blocking collectives: 132 us -> 46.5 us
  other arithmetic: 249 us -> 164 us
  waiting for transfers between devices: 88 us -> 170 us
    pallas_call x0 -> x2, Pallas kernels: none -> 159 us  [the longest x1 121 us: scan_backward(): pl.pallas_call(scan_back_kernel, grid=(count,), in_specs=[rows(INNER), ro...]
    dot_general x17 -> x14, matrix products: 297 us -> 161 us  [the longest x4 60.3 us: mm(): lax.dot_general(a, b, (((1,), (0,)), ((), ())), preferred_element_type=f32)]
    another operation x12 -> x1, other arithmetic: 96 us -> 0.04 us  [on_device(): jnp.stack([jnp.sum(pre_grad * padded[:, k:k + SEQ_LEN], axis=(0, 1)) for...]
    reshape x10 -> x6, local copies, waits for them, and re-layouts: 95.5 us -> 1.53 us  [the longest x1 0.76 us: gather_weights(): conv_weight.reshape(-1)]
    unnamed x3 -> x0, blocking collectives: 91.7 us -> none
    all_gather x2, waiting for transfers between devices: 0.02 us -> 72.6 us  [the longest x1 72.6 us: gather_weights(): lax.all_gather(jnp.concatenate([in_weight, side], axis=1), AXES, axis=0,...]
    convert_element_type x6 -> x9, other arithmetic: 44.7 us -> 96.7 us  [the longest x1 35.7 us: on_device(): act = jax.nn.silu(pre_act).astype(bf16).reshape(-1, CONVDIM)]
    reduce_sum x10 -> x8, other arithmetic: 102 us -> 56 us  [the longest x1 44.7 us: on_device(): conv_bias_grad = jnp.sum(pre_grad, axis=(0, 1))]
  transfers between devices with their start and end apart: 4 -> 5, of which waited for: 1 -> 2; matrix products, arithmetic and copies ran while one was open for 55% -> 42% of each run, Pallas kernels for 0% -> 22%
where the time goes in v1:
time: 742 us; the launch traced here: 736 us
  waiting for transfers between devices  170 us (23%)
  other arithmetic  164 us (22%)
  matrix products  161 us (22%)
  Pallas kernels  159 us (21%)
  blocking collectives  46.5 us (6%)
  local copies, waits for them, and re-layouts  20.9 us (3%)
  between operations  14.5 us (2%)
    pallas_call x1, Pallas kernels, scan_backward(): pl.pallas_call(scan_back_kernel, grid=(count,), in_specs=[rows(INNER), ro...  121 us
    reduce_scatter x1, waiting for transfers between devices, on_device(): lax.psum_scatter(late.astype(bf16), AXES, scatter_dimension=0, tiled=True)  96.6 us
    all_gather x1, waiting for transfers between devices, gather_weights(): lax.all_gather(jnp.concatenate([in_weight, side], axis=1), AXES, axis=0,...  72.6 us
    dot_general x4, matrix products, mm(): lax.dot_general(a, b, (((1,), (0,)), ((), ())), preferred_element_type=f32)  60.3 us
    dot_general x4, matrix products, mm_nt(): lax.dot_general(a, b, (((1,), (1,)), ((), ())), preferred_element_type=f32)  55.1 us
    reduce_sum x1, other arithmetic, on_device(): conv_bias_grad = jnp.sum(pre_grad, axis=(0, 1))  44.7 us
    dot_general x4, matrix products, mm_tn(): lax.dot_general(a, b, (((0,), (0,)), ((), ())), preferred_element_type=f32)  43.8 us
    psum x1, blocking collectives, on_device(): lax.psum(jnp.concatenate([conv_weight_grad.reshape(-1), conv_bias_grad, g...  40.3 us
  transfers between devices with their start and end apart: 5, of which 2 were waited for; matrix products, arithmetic and copies ran while one was open for 42% of the time, Pallas kernels for 22%

profile of v1, /device:TPU:0, one launch (start us, length us, event | category | flops | bytes accessed | tf_op | source)
XLA Modules:
  0.0 736.2 jit_solution(154571290255234563)
XLA Ops:
  7.2 0.8 reshape.143
  8.0 0.8 fusion.43
  8.8 1.7 pad_maximum_fusion.1
  10.7 0.7 all-gather.6.cloned.1.call-update
  11.4 3.1 fusion.10
  14.5 0.7 maximum_bitcast_fusion
  15.2 6.1 all-gather
  21.4 0.6 copy-done.30
  22.2 72.6 %all-gather.4.cloned.1.call-done = bf16[1024,4480]{1,0:T(8,128)(2,1)} async-done(((bf16[32,4480]{1,0:T(8,128)(2,1)}), bf16[1024,4480]{1,0:T(8,128)(2,1)}) %all-gather.4.cloned.1.call-update) | async-done | bytes 9175056 | tf_op jit(solution)/shard_map/all_gather | solution.py:243
  94.8 1.1 slice.115
  95.9 0.3 reshape.145
  96.6 0.2 slice_reduce_fusion.5
  97.3 5.0 compare_select_fusion
  102.3 1.0 fusion.33.cum_t_ref
  103.2 0.3 copy.98
  103.6 0.3 copy.100
  104.0 17.1 %fusion.15 = f32[2048,2304]{1,0:T(8,128)} fusion(bf16[1024,4480]{1,0:T(8,128)(2,1)} %all-gather.4.cloned.1.call-done, bf16[2048,1024]{1,0:T(8,128)(2,1)} %param.11, f32[1024]{0:T(1024)S(1)} %reshape.161, f32[2048]{0:T(1024)S(1)} %add_rsqrt_fusion.1), kind=kOutput, calls=%fused_computation.42 | convolution fusion | flops 9672065024 | bytes 27799552 | tf_op jit(solution)/shard_map/dot_general | solution.py:30
  121.1 35.7 %multiply_convert_fusion = (bf16[2,1024,2304]{2,1,0:T(8,128)(2,1)}, f32[2,1024,2304]{2,1,0:T(8,128)}) fusion(f32[2,1024,2304]{2,1,0:T(8,128)} %bitcast.104, f32[2304]{0:T(1024)S(1)} %mul.293, f32[2304]{0:T(1024)S(1)} %mul.290, f32[2304]{0:T(1024)S(1)} %mul.287, f32[2304]{0:T(1024)S(1)} %mul.279, f32[2304]{0:T(1024)S(1)} %reshape.160), kind=kLoop, calls=%fused_computation.8 | loop fusion | flops 61341696 | bytes 47232000 | tf_op jit(solution)/shard_map/convert_element_type | solution.py:287
  156.9 37.7 %shard_map.194 = (f32[2048,2048]{1,0:T(8,128)}, bf16[8,128,2048]{2,1,0:T(8,128)(2,1)S(1)}) custom-call(bf16[2048,2304]{1,0:T(8,128)(2,1)} %bitcast.106, f32[2048,32]{1,0:T(8,128)S(1)} %bitcast.99, f32[2048,32]{1,0:T(8,128)S(1)} %get-tuple-element.53.step_ref, f32[8,32,256]{2,1,0:T(8,128)S(1)} %fusion.33.cum_t_ref, f32[8,32,256]{2,1,0:T(8,128)S(1)} %bitcast.101, ...), custom_call_target="tpu_custom_call" | custom-call | flops 16000000000 | bytes 30720000 | tf_op jit(solution)/shard_map/pallas_call | solution.py:178
  194.6 2.0 copy-done.6
  196.6 22.8 %multiply_reduce_fusion.6 = (f32[2048]{0:T(1024)S(1)}, f32[2048,2048]{1,0:T(8,128)}, f32[2048,2048]{1,0:T(8,128)}) fusion(f32[2048,2048]{1,0:T(8,128)} %get-tuple-element.18, bf16[1024,4480]{1,0:T(8,128)(2,1)} %all-gather.4.cloned.1.call-done, bf16[2048,1024]{1,0:T(8,128)(2,1)S(1)} %copy-done.8, f32[1024]{0:T(1024)S(1)} %reshape.161, ...), kind=kOutput, calls=%fused_computation.19 | convolution fusion | flops 8627681280 | bytes 58740736 | tf_op jit(solution)/shard_map/dot_general | solution.py:30
  219.5 14.7 %convolution_convert_fusion.2 = bf16[2048,1024]{0,1:T(8,128)(2,1)} fusion(bf16[2048,1024]{1,0:T(8,128)(2,1)S(1)} %copy-done.13, f32[2048,2048]{1,0:T(8,128)} %get-tuple-element.47, f32[2048]{0:T(1024)S(1)} %reshape.162, f32[2048]{0:T(1024)S(1)} %add_rsqrt_fusion), kind=kOutput, calls=%fused_computation.45 | convolution fusion | flops 8604614656 | bytes 25182208 | tf_op jit(solution)/shard_map/dot_general | solution.py:38
  234.2 18.4 %multiply_reduce_fusion.4 = (f32[2048]{0:T(1024)S(1)}, f32[2048]{0:T(1024)S(1)}, f32[2048,2048]{1,0:T(8,128)}) fusion(f32[2048,2048]{1,0:T(8,128)} %get-tuple-element.47, f32[2048]{0:T(1024)S(1)} %add_rsqrt_fusion, f32[2048]{0:T(1024)S(1)} %reshape.162, bf16[2048,1024]{1,0:T(8,128)(2,1)} %param.21, bf16[2048,1024]{0,1:T(8,128)(2,1)} %all-gather.6.cloned.1.call-done), kind=kOutput, calls=%fused_computation.13 | convolution fusion | flops 8615096320 | bytes 41975808 | tf_op jit(solution)/shard_map/dot_general | solution.py:34
  252.7 30.2 %multiply_convert_fusion.1 = (bf16[2048,2048]{1,0:T(8,128)(2,1)}, bf16[2048,2048]{1,0:T(8,128)(2,1)}) fusion(f32[2048]{0:T(1024)S(1)} %broadcast_multiply_fusion.1, f32[2048,2048]{1,0:T(8,128)} %get-tuple-element.47, f32[2048,2048]{1,0:T(8,128)} %get-tuple-element.63, f32[2048]{0:T(1024)S(1)} %reshape.162, f32[2048]{0:T(1024)S(1)} %add_rsqrt_fusion, ...), kind=kLoop, calls=%fused_computation.14 | loop fusion | flops 79691776 | bytes 83910656 | tf_op jit(solution)/shard_map/convert_element_type | solution.py:311
  282.9 1.4 copy.97
  284.3 0.9 copy-done.3
  285.3 2.2 copy-done.7
  287.4 121.2 %shard_map.195 = (f32[2048,2304]{1,0:T(8,128)}, f32[2048,32]{1,0:T(8,128)S(1)}, f32[2048,32]{1,0:T(8,128)S(1)}, f32[8,32,256]{2,1,0:T(8,128)S(1)}, f32[8,8,2048]{2,1,0:T(8,128)S(1)}) custom-call(bf16[2048,2048]{1,0:T(8,128)(2,1)} %get-tuple-element.50.dy_ref, bf16[2048,2304]{1,0:T(8,128)(2,1)} %bitcast.107, bf16[8,128,2048]{2,1,0:T(8,128)(2,1)S(1)} %copy-done.7, ...), custom_call_target="tpu_custom_call" | custom-call | flops 32000000000 | bytes 40960000 | tf_op jit(solution)/shard_map/pallas_call | solution.py:200
  408.6 1.0 copy-done
  409.6 0.7 copy-done.4
  410.3 0.8 copy-done.5
  411.1 2.4 copy.106
  413.5 0.7 slice_bitcast_fusion
  414.2 1.4 subtract_exponential_fusion
  415.5 0.2 copy.107
  415.7 1.4 slice_reduce_fusion
  417.4 2.0 bitcast_reduce_fusion
  419.4 0.7 fusion.45
  420.1 2.3 fusion.27
  422.4 1.0 fusion.22
  423.4 0.3 copy.109
  423.7 2.7 fusion.54
  426.4 0.8 copy-done.15
  427.2 3.5 convolution_convert_fusion.3
  430.8 14.8 %convolution_convert_fusion.1 = bf16[1024,2048]{1,0:T(8,128)(2,1)} fusion(bf16[2048,2048]{1,0:T(8,128)(2,1)} %get-tuple-element.51, bf16[2048,1024]{1,0:T(8,128)(2,1)} %param.11, f32[1024]{0:T(1024)S(1)} %reshape.161, f32[2048]{0:T(1024)S(1)} %add_rsqrt_fusion.1), kind=kOutput, calls=%fused_computation.44 | convolution fusion | flops 8600420352 | bytes 16789504 | tf_op jit(solution)/shard_map/dot_general | solution.py:38
  445.8 44.7 %fusion.53 = (f32[2304]{0:T(1024)S(1)}, f32[2304]{0:T(1024)S(1)}, f32[2304]{0:T(1024)S(1)}, f32[2304]{0:T(1024)S(1)}, f32[2304]{0:T(1024)S(1)}, /*index=5*/f32[2,1024,2304]{2,1,0:T(8,128)}) fusion(f32[2048,2304]{1,0:T(8,128)} %fusion.15, f32[2,1024,2304]{2,1,0:T(8,128)} %bitcast.105, f32[2,1024,2304]{2,1,0:T(8,128)} %get-tuple-element.49, ...), kind=kLoop, calls=%fused_computation.114 | loop fusion | flops 80204544 | bytes 94417920 | tf_op jit(solution)/shard_map/reduce_sum | solution.py:338
  490.8 0.7 fusion.46
  491.5 25.0 %add_convert_fusion = bf16[2,1024,2304]{2,1,0:T(8,128)(2,1)S(1)} fusion(f32[2,1024,2304]{2,1,0:T(8,128)} %get-tuple-element.45, f32[2304]{0:T(1024)S(1)} %copy-done.19, f32[2304]{0:T(1024)S(1)} %copy-done.21, f32[2304]{0:T(1024)S(1)} %copy-done.23, f32[2304]{0:T(1024)S(1)} %copy-done.25), kind=kLoop, calls=%fused_computation.4 | loop fusion | flops 37748736 | bytes 28348416 | tf_op jit(solution)/shard_map/convert_element_type | solution.py:346
  516.6 10.7 %convolution_convert_fusion = bf16[1024,2304]{1,0:T(8,128)(2,1)S(1)} fusion(bf16[2048,2304]{1,0:T(8,128)(2,1)S(1)} %bitcast.108, bf16[2048,1024]{1,0:T(8,128)(2,1)S(1)} %copy-done.9, f32[1024]{0:T(1024)S(1)} %reshape.161, f32[2048]{0:T(1024)S(1)} %add_rsqrt_fusion.1), kind=kOutput, calls=%fused_computation.38 | convolution fusion | flops 9674424320 | bytes 18362368 | tf_op jit(solution)/shard_map/dot_general | solution.py:38
  527.4 2.5 pad_maximum_fusion
  530.0 40.3 %psum.7 = f32[13664]{0:T(1024)S(1)} all-reduce(f32[13664]{0:T(1024)S(1)} %concatenate.20), channel_id=1, replica_groups=mesh['dp'=8,'fsdp'=4] {'dp','fsdp'}, use_global_device_ids=true, to_apply=%region_19.20 | all-reduce | flops 13664 | bytes 109312 | tf_op jit(solution)/shard_map/psum | solution.py:361
  570.4 0.6 dynamic_slice.19
  571.0 0.6 dynamic_slice.20
  571.6 0.6 fusion.57
  572.2 0.6 constant_dynamic-slice_fusion
  572.8 14.6 %fusion.17 = f32[2048,1024]{1,0:T(8,128)} fusion(bf16[2048,2048]{1,0:T(8,128)(2,1)} %get-tuple-element.51, bf16[1024,4480]{1,0:T(8,128)(2,1)} %all-gather.4.cloned.1.call-done), kind=kOutput, calls=%fused_computation.46 | convolution fusion | flops 8589934592 | bytes 20971520 | tf_op jit(solution)/shard_map/dot_general | solution.py:34
  587.5 14.6 %fusion.13 = f32[2048,1024]{1,0:T(8,128)} fusion(bf16[2048,2304]{1,0:T(8,128)(2,1)S(1)} %bitcast.109, bf16[1024,4480]{1,0:T(8,128)(2,1)} %all-gather.4.cloned.1.call-done), kind=kOutput, calls=%fused_computation.40 | convolution fusion | flops 9663676416 | bytes 22544384 | tf_op jit(solution)/shard_map/dot_general | solution.py:34
  602.1 7.4 %fusion.12 = (f32[2048]{0:T(1024)S(1)}, f32[2048,1024]{1,0:T(8,128)S(1)}) fusion(bf16[2048,1024]{1,0:T(8,128)(2,1)S(1)} %copy-done.10, f32[1024]{0:T(1024)S(1)} %reshape.161, bf16[1024,4480]{1,0:T(8,128)(2,1)} %all-gather.4.cloned.1.call-done, bf16[2048,32]{1,0:T(8,128)(2,1)S(1)} %copy-done.16, f32[2048,1024]{1,0:T(8,128)} %fusion.17, f32[2048,1024]{1,0:T(8,128)} %fusion.13), kind=kOutput, calls=%fused_computation.36 | convolution fusion | flops 146798592 | bytes 29765632 | tf_op jit(solution)/shard_map/dot_general | solution.py:34
  609.6 3.8 fusion.9
  613.4 15.3 %fusion.11 = bf16[2048,1024]{1,0:T(8,128)(2,1)} fusion(bf16[2048,1024]{1,0:T(8,128)(2,1)S(1)} %copy-done.10, bf16[2048,1024]{0,1:T(8,128)(2,1)} %all-gather.6.cloned.1.call-done, f32[2048,2048]{1,0:T(8,128)} %get-tuple-element.47, f32[2048]{0:T(1024)S(1)} %copy-done.27, f32[2048]{0:T(1024)S(1)} %copy-done.29), kind=kOutput, calls=%fused_computation.35 | convolution fusion | flops 8608808960 | bytes 29376512 | tf_op jit(solution)/shard_map/dot_general | solution.py:30
  628.7 1.6 convert_element_type.123
  630.4 96.6 %reduce-scatter.6.cloned.1.call-done = bf16[32,2336]{1,0:T(8,128)(2,1)} async-done(((bf16[1024,2336]{1,0:T(8,128)(2,1)}), bf16[32,2336]{1,0:T(8,128)(2,1)}) %reduce-scatter.6.cloned.1.call-update) | async-done | bytes 149520 | tf_op jit(solution)/shard_map/reduce_scatter | solution.py:349
  726.9 2.0 multiply_reduce_fusion.7
  728.9 0.5 convert_divide_fusion
  (108 shorter events, 2.4 us)
Async XLA Ops:
  7.2 87.6 %all-gather.4.cloned.1.call-start = ((), (), s32[]{:S(2)}) async-start(), calls=%async_computation.3 | async-start | bytes 9461760 | tf_op jit(solution)/shard_map/all_gather | solution.py:243
  10.6 223.5 %all-gather.6.cloned.1.call-start = ((), (), s32[]{:S(2)}) async-start(), calls=%async_computation.4 | async-start | bytes 4325376 | tf_op jit(solution)/shard_map/all_gather | solution.py:264
  11.4 617.4 %reduce-scatter.8.cloned.1.call-start = ((), (), s32[]{:S(2)}) async-start(), calls=%async_computation.7 | async-start | bytes 4325376 | tf_op jit(solution)/shard_map/reduce_scatter | solution.py:300
  21.4 0.6 copy-start.30
  22.0 80.3 %copy-start.31 = (f32[32]{0:T(128)}, f32[32]{0:T(128)S(1)}, u32[]{:S(2)}) copy-start(f32[32]{0:T(128)S(1)} %get-tuple-element.59) | copy-start | bytes 388
  96.9 24.2 %copy-start.18 = (f32[2304]{0:T(1024)}, f32[2304]{0:T(1024)S(1)}, u32[]{:S(2)}) copy-start(f32[2304]{0:T(1024)S(1)} %mul.293) | copy-start | bytes 27652
  97.0 24.1 %copy-start.20 = (f32[2304]{0:T(1024)}, f32[2304]{0:T(1024)S(1)}, u32[]{:S(2)}) copy-start(f32[2304]{0:T(1024)S(1)} %mul.290) | copy-start | bytes 27652
  97.1 24.0 %copy-start.22 = (f32[2304]{0:T(1024)}, f32[2304]{0:T(1024)S(1)}, u32[]{:S(2)}) copy-start(f32[2304]{0:T(1024)S(1)} %mul.287) | copy-start | bytes 27652
  97.2 23.9 %copy-start.24 = (f32[2304]{0:T(1024)}, f32[2304]{0:T(1024)S(1)}, u32[]{:S(2)}) copy-start(f32[2304]{0:T(1024)S(1)} %mul.279) | copy-start | bytes 27652
  103.9 53.0 %copy-start.2 = (f32[8,256,32]{1,2,0:T(8,128)}, f32[8,256,32]{1,2,0:T(8,128)S(1)}, u32[]{:S(2)}) copy-start(f32[8,256,32]{1,2,0:T(8,128)S(1)} %copy.100) | copy-start | bytes 786436
  104.0 148.7 %copy-start.26 = (f32[2048]{0:T(1024)}, f32[2048]{0:T(1024)S(1)}, u32[]{:S(2)}) copy-start(f32[2048]{0:T(1024)S(1)} %reshape.162) | copy-start | bytes 24580
  156.9 39.7 %copy-start.8 = (bf16[2048,1024]{1,0:T(8,128)(2,1)S(1)}, bf16[2048,1024]{1,0:T(8,128)(2,1)}, u32[]{:S(2)}) copy-start(bf16[2048,1024]{1,0:T(8,128)(2,1)} %param.11) | copy-start | bytes 12582916
  194.6 2.0 copy-start.6
  196.6 22.9 %copy-start.13 = (bf16[2048,1024]{1,0:T(8,128)(2,1)S(1)}, bf16[2048,1024]{1,0:T(8,128)(2,1)}, u32[]{:S(2)}) copy-start(bf16[2048,1024]{1,0:T(8,128)(2,1)} %param.21) | copy-start | bytes 12582916
  219.4 33.2 %copy-start.28 = (f32[2048]{0:T(1024)}, f32[2048]{0:T(1024)S(1)}, u32[]{:S(2)}) copy-start(f32[2048]{0:T(1024)S(1)} %add_rsqrt_fusion) | copy-start | bytes 24580
  252.6 377.7 %reduce-scatter.4.cloned.1.call-start = ((), (), s32[]{:S(2)}) async-start(), calls=%async_computation.5 | async-start | bytes 4325376 | tf_op jit(solution)/shard_map/reduce_scatter | solution.py:313
  284.3 1.0 copy-start.3
  285.3 2.2 copy-start.7
  408.6 1.0 copy-start
  409.6 0.7 copy-start.4
  410.3 0.8 copy-start.5
  411.1 12.6 %copy-start.32 = (f32[32]{0:T(128)S(1)}, f32[32]{0:T(128)}, u32[]{:S(2)}) copy-start(f32[32]{0:T(128)} %copy-done.31) | copy-start | bytes 388
  411.1 9.0 %copy-start.1 = (f32[2048,32]{1,0:T(8,128)S(1)}, f32[2048,32]{1,0:T(8,128)}, u32[]{:S(2)}) copy-start(f32[2048,32]{1,0:T(8,128)} %copy-done) | copy-start | bytes 786436
  426.4 0.8 copy-start.15
  445.7 281.2 %reduce-scatter.6.cloned.1.call-start = ((), (), s32[]{:S(2)}) async-start(), calls=%async_computation.6 | async-start | bytes 5136384 | tf_op jit(solution)/shard_map/reduce_scatter | solution.py:349
  445.8 45.7 %copy-start.19 = (f32[2304]{0:T(1024)S(1)}, f32[2304]{0:T(1024)}, u32[]{:S(2)}) copy-start(f32[2304]{0:T(1024)} %copy-done.18) | copy-start | bytes 27652
  445.8 45.7 %copy-start.21 = (f32[2304]{0:T(1024)S(1)}, f32[2304]{0:T(1024)}, u32[]{:S(2)}) copy-start(f32[2304]{0:T(1024)} %copy-done.20) | copy-start | bytes 27652
  445.8 45.7 %copy-start.23 = (f32[2304]{0:T(1024)S(1)}, f32[2304]{0:T(1024)}, u32[]{:S(2)}) copy-start(f32[2304]{0:T(1024)} %copy-done.22) | copy-start | bytes 27652
  445.8 45.7 %copy-start.25 = (f32[2304]{0:T(1024)S(1)}, f32[2304]{0:T(1024)}, u32[]{:S(2)}) copy-start(f32[2304]{0:T(1024)} %copy-done.24) | copy-start | bytes 27652
  491.5 25.1 %copy-start.9 = (bf16[2048,1024]{1,0:T(8,128)(2,1)S(1)}, bf16[2048,1024]{1,0:T(8,128)(2,1)}, u32[]{:S(2)}) copy-start(bf16[2048,1024]{1,0:T(8,128)(2,1)} %param.11) | copy-start | bytes 12582916
  516.6 10.8 %copy-start.11 = (bf16[2,1024,2304]{2,1,0:T(8,128)(2,1)}, bf16[2,1024,2304]{2,1,0:T(8,128)(2,1)S(1)}, u32[]{:S(2)}) copy-start(bf16[2,1024,2304]{2,1,0:T(8,128)(2,1)S(1)} %add_convert_fusion) | copy-start | bytes 28311556
  572.8 14.6 %copy-start.12 = (bf16[2,1024,2304]{2,1,0:T(8,128)(2,1)S(1)}, bf16[2,1024,2304]{2,1,0:T(8,128)(2,1)}, u32[]{:S(2)}) copy-start(bf16[2,1024,2304]{2,1,0:T(8,128)(2,1)} %copy-done.11) | copy-start | bytes 28311556
  587.5 14.7 %copy-start.10 = (bf16[2048,1024]{1,0:T(8,128)(2,1)S(1)}, bf16[2048,1024]{1,0:T(8,128)(2,1)}, u32[]{:S(2)}) copy-start(bf16[2048,1024]{1,0:T(8,128)(2,1)} %param.11) | copy-start | bytes 12582916
  587.5 14.7 %copy-start.16 = (bf16[2048,32]{1,0:T(8,128)(2,1)S(1)}, bf16[2048,32]{1,0:T(8,128)(2,1)}, u32[]{:S(2)}) copy-start(bf16[2048,32]{1,0:T(8,128)(2,1)} %copy-done.15) | copy-start | bytes 393220
  602.1 7.4 %copy-start.14 = (bf16[2048,1024]{1,0:T(8,128)(2,1)S(1)}, bf16[2048,1024]{1,0:T(8,128)(2,1)}, u32[]{:S(2)}) copy-start(bf16[2048,1024]{1,0:T(8,128)(2,1)} %param.21) | copy-start | bytes 12582916
  609.5 3.8 copy-start.27
  609.6 3.8 copy-start.29
  613.4 113.5 %copy-start.17 = (bf16[32,4384]{1,0:T(8,128)(2,1)S(1)}, bf16[32,4384]{1,0:T(8,128)(2,1)}, u32[]{:S(2)}) copy-start(bf16[32,4384]{1,0:T(8,128)(2,1)} %param.12) | copy-start | bytes 841732
  613.4 115.5 %copy-start.33 = (bf16[32]{0:T(256)(128)(2,1)S(1)}, bf16[32]{0:T(256)(128)(2,1)}, u32[]{:S(2)}) copy-start(bf16[32]{0:T(256)(128)(2,1)} %param.16) | copy-start | bytes 196
Sparse Core Ops, SparseCore 0:
  11.4 83.2 all-gather.3
  97.6 60.6 all-gather.5
  252.7 140.4 reduce-scatter.7
  445.8 140.3 reduce-scatter.3
  588.3 138.5 reduce-scatter.5

commit v2 on v1

--- a/solution.py
+++ b/solution.py
@@ -261,6 +261,7 @@
     whole, taps, bias_all, norm_all, gate_all = gather_weights(
         in_weight, conv_weight, conv_bias, norm_gain, gate_gain
     )
+    whole, out_weight = lax.optimization_barrier((whole, out_weight))
     out_all = lax.all_gather(out_weight, AXES, axis=1, tiled=True)
     head_all = lax.all_gather(
         jnp.stack([decay_log, step_bias, skip_scale]), "fsdp", axis=1, tiled=True

time: 742 us -> 744 us (level)
  transfers between devices with their start and end apart: 5 -> 5, of which waited for: 2 -> 2; matrix products, arithmetic and copies ran while one was open for 42% -> 45% of each run, Pallas kernels for 22% -> 22%
where the time goes in v2:
time: 744 us; the launch traced here: 735 us
  waiting for transfers between devices  170 us (23%)
  other arithmetic  167 us (22%)
  matrix products  160 us (22%)
  Pallas kernels  159 us (21%)
  blocking collectives  46.5 us (6%)
  local copies, waits for them, and re-layouts  18.8 us (3%)
  between operations  14.5 us (2%)
    pallas_call x1, Pallas kernels, scan_backward(): pl.pallas_call(scan_back_kernel, grid=(count,), in_specs=[rows(INNER), ro...  121 us
    reduce_scatter x1, waiting for transfers between devices, on_device(): lax.psum_scatter(late.astype(bf16), AXES, scatter_dimension=0, tiled=True)  96.2 us
    all_gather x1, waiting for transfers between devices, gather_weights(): lax.all_gather(jnp.concatenate([in_weight, side], axis=1), AXES, axis=0,...  73.3 us
    dot_general x4, matrix products, mm(): lax.dot_general(a, b, (((1,), (0,)), ((), ())), preferred_element_type=f32)  58.4 us
    dot_general x4, matrix products, mm_nt(): lax.dot_general(a, b, (((1,), (1,)), ((), ())), preferred_element_type=f32)  55.2 us
    reduce_sum x1, other arithmetic, on_device(): conv_bias_grad = jnp.sum(pre_grad, axis=(0, 1))  44.7 us
    dot_general x4, matrix products, mm_tn(): lax.dot_general(a, b, (((0,), (0,)), ((), ())), preferred_element_type=f32)  44.1 us
    psum x1, blocking collectives, on_device(): lax.psum(jnp.concatenate([conv_weight_grad.reshape(-1), conv_bias_grad, g...  40.4 us
  transfers between devices with their start and end apart: 5, of which 2 were waited for; matrix products, arithmetic and copies ran while one was open for 45% of the time, Pallas kernels for 22%

profile of v2, /device:TPU:0, one launch (start us, length us, event | category | flops | bytes accessed | tf_op | source)
XLA Modules:
  0.0 735.2 jit_solution(9851481346785000425)
XLA Ops:
  7.2 0.8 reshape.143
  8.0 0.8 fusion.45
  8.8 1.7 pad_maximum_fusion.1
  10.7 0.7 maximum_bitcast_fusion
  11.4 6.1 all-gather
  17.6 0.6 copy-done.31
  18.3 3.1 fusion.12
  21.4 73.3 %all-gather.4.cloned.1.call-done = bf16[1024,4480]{1,0:T(8,128)(2,1)} async-done(((bf16[32,4480]{1,0:T(8,128)(2,1)}), bf16[1024,4480]{1,0:T(8,128)(2,1)}) %all-gather.4.cloned.1.call-update) | async-done | bytes 9175056 | tf_op jit(solution)/shard_map/all_gather | solution.py:243
  94.8 1.1 slice.115
  95.8 0.3 reshape.145
  96.7 0.2 slice_reduce_fusion.5
  97.4 17.0 %fusion.17 = f32[2048,2304]{1,0:T(8,128)} fusion(bf16[1024,4480]{1,0:T(8,128)(2,1)} %all-gather.4.cloned.1.call-done, bf16[2048,1024]{1,0:T(8,128)(2,1)} %param.11, f32[1024]{0:T(1024)S(1)} %reshape.161, f32[2048]{0:T(1024)S(1)} %add_rsqrt_fusion.1), kind=kOutput, calls=%fused_computation.45 | convolution fusion | flops 9672065024 | bytes 27799552 | tf_op jit(solution)/shard_map/dot_general | solution.py:30
  114.4 3.8 compare_select_fusion
  118.1 1.0 fusion.35.cum_t_ref
  119.1 1.3 copy.101
  120.4 0.3 copy.102
  120.8 0.3 copy.104
  121.2 0.7 slice_bitcast_fusion
  121.9 1.4 subtract_exponential_fusion
  123.2 1.2 copy.112
  124.5 36.7 %multiply_convert_fusion = (bf16[2,1024,2304]{2,1,0:T(8,128)(2,1)}, f32[2,1024,2304]{2,1,0:T(8,128)}) fusion(f32[2,1024,2304]{2,1,0:T(8,128)} %bitcast.119, f32[2304]{0:T(1024)S(1)} %mul.293, f32[2304]{0:T(1024)S(1)} %mul.290, f32[2304]{0:T(1024)S(1)} %mul.287, f32[2304]{0:T(1024)S(1)} %mul.279, f32[2304]{0:T(1024)S(1)} %reshape.160), kind=kLoop, calls=%fused_computation.8 | loop fusion | flops 61341696 | bytes 47232000 | tf_op jit(solution)/shard_map/convert_element_type | solution.py:288
  161.2 37.9 %shard_map.194 = (f32[2048,2048]{1,0:T(8,128)}, bf16[8,128,2048]{2,1,0:T(8,128)(2,1)S(1)}) custom-call(bf16[2048,2304]{1,0:T(8,128)(2,1)} %bitcast.121, f32[2048,32]{1,0:T(8,128)S(1)} %bitcast.114, f32[2048,32]{1,0:T(8,128)S(1)} %get-tuple-element.57.step_ref, f32[8,32,256]{2,1,0:T(8,128)S(1)} %fusion.35.cum_t_ref, f32[8,32,256]{2,1,0:T(8,128)S(1)} %bitcast.116, ...), custom_call_target="tpu_custom_call" | custom-call | flops 16000000000 | bytes 30720000 | tf_op jit(solution)/shard_map/pallas_call | solution.py:178
  199.1 2.0 copy-done.5
  201.1 22.3 %multiply_reduce_fusion.5 = (f32[2048]{0:T(1024)S(1)}, f32[2048,2048]{1,0:T(8,128)}, f32[2048,2048]{1,0:T(8,128)}) fusion(f32[2048,2048]{1,0:T(8,128)} %get-tuple-element.21, bf16[1024,4480]{1,0:T(8,128)(2,1)} %all-gather.4.cloned.1.call-done, bf16[2048,1024]{1,0:T(8,128)(2,1)S(1)} %copy-done.8, f32[1024]{0:T(1024)S(1)} %reshape.161, ...), kind=kOutput, calls=%fused_computation.22 | convolution fusion | flops 8627681280 | bytes 58740736 | tf_op jit(solution)/shard_map/dot_general | solution.py:30
  223.4 15.1 %convolution_convert_fusion.2 = bf16[2048,1024]{0,1:T(8,128)(2,1)} fusion(bf16[2048,1024]{1,0:T(8,128)(2,1)S(1)} %copy-done.14, f32[2048,2048]{1,0:T(8,128)} %get-tuple-element.51, f32[2048]{0:T(1024)S(1)} %reshape.162, f32[2048]{0:T(1024)S(1)} %add_rsqrt_fusion), kind=kOutput, calls=%fused_computation.48 | convolution fusion | flops 8604614656 | bytes 25182208 | tf_op jit(solution)/shard_map/dot_general | solution.py:38
  238.6 18.5 %fusion.2 = (f32[2048]{0:T(1024)S(1)}, f32[2048]{0:T(1024)S(1)}, f32[2048,2048]{0,1:T(8,128)}) fusion(f32[2048,2048]{1,0:T(8,128)} %get-tuple-element.51, f32[2048]{0:T(1024)S(1)} %add_rsqrt_fusion, f32[2048]{0:T(1024)S(1)} %reshape.162, bf16[2048,1024]{1,0:T(8,128)(2,1)} %param.21, bf16[2048,1024]{0,1:T(8,128)(2,1)} %all-gather.6.cloned.1.call-done), kind=kOutput, calls=%fused_computation.16 | convolution fusion | flops 8615096320 | bytes 41975808 | tf_op jit(solution)/shard_map/dot_general | solution.py:34
  257.2 31.1 %multiply_convert_fusion.1 = (bf16[2048,2048]{1,0:T(8,128)(2,1)}, bf16[2048,2048]{1,0:T(8,128)(2,1)}) fusion(f32[2048]{0:T(1024)S(1)} %broadcast_multiply_fusion.1, f32[2048,2048]{1,0:T(8,128)} %get-tuple-element.51, f32[2048,2048]{0,1:T(8,128)} %get-tuple-element.67, f32[2048]{0:T(1024)S(1)} %reshape.162, f32[2048]{0:T(1024)S(1)} %add_rsqrt_fusion, ...), kind=kLoop, calls=%fused_computation.17 | loop fusion | flops 79691776 | bytes 83910656 | tf_op jit(solution)/shard_map/convert_element_type | solution.py:312
  288.3 121.3 %shard_map.195 = (f32[2048,2304]{1,0:T(8,128)}, f32[2048,32]{1,0:T(8,128)S(1)}, f32[2048,32]{1,0:T(8,128)S(1)}, f32[8,32,256]{2,1,0:T(8,128)S(1)}, f32[8,8,2048]{2,1,0:T(8,128)S(1)}) custom-call(bf16[2048,2048]{1,0:T(8,128)(2,1)} %get-tuple-element.54.dy_ref, bf16[2048,2304]{1,0:T(8,128)(2,1)} %bitcast.122, bf16[8,128,2048]{2,1,0:T(8,128)(2,1)S(1)} %copy-done.6, ...), custom_call_target="tpu_custom_call" | custom-call | flops 32000000000 | bytes 40960000 | tf_op jit(solution)/shard_map/pallas_call | solution.py:200
  409.7 1.0 copy-done
  410.6 0.7 copy-done.3
  411.3 0.8 copy-done.4
  412.1 1.4 copy.111
  413.5 1.4 slice_reduce_fusion
  415.0 0.1 reduce_sum.160
  415.1 2.2 bitcast_reduce_fusion
  417.4 0.7 fusion.47
  418.1 2.7 fusion.29
  420.8 1.0 fusion.24
  421.8 1.3 copy.114
  423.1 2.6 fusion.56
  425.7 0.8 copy-done.16
  426.5 3.5 convolution_convert_fusion.3
  430.0 0.2 copy.116
  430.2 14.8 %convolution_convert_fusion.1 = bf16[1024,2048]{1,0:T(8,128)(2,1)} fusion(bf16[2048,2048]{1,0:T(8,128)(2,1)} %get-tuple-element.55, bf16[2048,1024]{1,0:T(8,128)(2,1)} %param.11, f32[1024]{0:T(1024)S(1)} %reshape.161, f32[2048]{0:T(1024)S(1)} %add_rsqrt_fusion.1), kind=kOutput, calls=%fused_computation.47 | convolution fusion | flops 8600420352 | bytes 16789504 | tf_op jit(solution)/shard_map/dot_general | solution.py:38
  445.1 44.7 %fusion.55 = (f32[2304]{0:T(1024)S(1)}, f32[2304]{0:T(1024)S(1)}, f32[2304]{0:T(1024)S(1)}, f32[2304]{0:T(1024)S(1)}, f32[2304]{0:T(1024)S(1)}, /*index=5*/f32[2,1024,2304]{2,1,0:T(8,128)}) fusion(f32[2048,2304]{1,0:T(8,128)} %fusion.17, f32[2,1024,2304]{2,1,0:T(8,128)} %bitcast.120, f32[2,1024,2304]{2,1,0:T(8,128)} %get-tuple-element.53, ...), kind=kLoop, calls=%fused_computation.117 | loop fusion | flops 80204544 | bytes 94417920 | tf_op jit(solution)/shard_map/reduce_sum | solution.py:339
  490.0 0.1 reduce_sum.173
  490.1 0.7 fusion.48
  490.9 25.0 %add_convert_fusion = bf16[2,1024,2304]{2,1,0:T(8,128)(2,1)S(1)} fusion(f32[2,1024,2304]{2,1,0:T(8,128)} %get-tuple-element.49, f32[2304]{0:T(1024)S(1)} %copy-done.20, f32[2304]{0:T(1024)S(1)} %copy-done.22, f32[2304]{0:T(1024)S(1)} %copy-done.24, f32[2304]{0:T(1024)S(1)} %copy-done.26), kind=kLoop, calls=%fused_computation.4 | loop fusion | flops 37748736 | bytes 28348416 | tf_op jit(solution)/shard_map/convert_element_type | solution.py:347
  515.9 10.7 %convolution_convert_fusion = bf16[1024,2304]{1,0:T(8,128)(2,1)S(1)} fusion(bf16[2048,2304]{1,0:T(8,128)(2,1)S(1)} %bitcast.123, bf16[2048,1024]{1,0:T(8,128)(2,1)S(1)} %copy-done.9, f32[1024]{0:T(1024)S(1)} %reshape.161, f32[2048]{0:T(1024)S(1)} %add_rsqrt_fusion.1), kind=kOutput, calls=%fused_computation.41 | convolution fusion | flops 9674424320 | bytes 18362368 | tf_op jit(solution)/shard_map/dot_general | solution.py:38
  526.7 2.5 pad_maximum_fusion
  529.3 40.4 %psum.7 = f32[13664]{0:T(1024)S(1)} all-reduce(f32[13664]{0:T(1024)S(1)} %concatenate.20), channel_id=1, replica_groups=mesh['dp'=8,'fsdp'=4] {'dp','fsdp'}, use_global_device_ids=true, to_apply=%region_19.20 | all-reduce | flops 13664 | bytes 109312 | tf_op jit(solution)/shard_map/psum | solution.py:362
  569.8 0.6 dynamic_slice.19
  570.4 0.6 dynamic_slice.20
  571.0 0.6 fusion.59
  571.6 0.6 constant_dynamic-slice_fusion
  572.2 14.6 %fusion.19 = f32[2048,1024]{1,0:T(8,128)} fusion(bf16[2048,2048]{1,0:T(8,128)(2,1)} %get-tuple-element.55, bf16[1024,4480]{1,0:T(8,128)(2,1)} %all-gather.4.cloned.1.call-done), kind=kOutput, calls=%fused_computation.49 | convolution fusion | flops 8589934592 | bytes 20971520 | tf_op jit(solution)/shard_map/dot_general | solution.py:34
  586.9 14.6 %fusion.15 = f32[2048,1024]{1,0:T(8,128)} fusion(bf16[2048,2304]{1,0:T(8,128)(2,1)S(1)} %bitcast.124, bf16[1024,4480]{1,0:T(8,128)(2,1)} %all-gather.4.cloned.1.call-done), kind=kOutput, calls=%fused_computation.43 | convolution fusion | flops 9663676416 | bytes 22544384 | tf_op jit(solution)/shard_map/dot_general | solution.py:34
  601.5 7.4 %fusion.14 = (f32[2048]{0:T(1024)S(1)}, f32[2048,1024]{1,0:T(8,128)S(1)}) fusion(bf16[2048,1024]{1,0:T(8,128)(2,1)S(1)} %copy-done.10, f32[1024]{0:T(1024)S(1)} %reshape.161, bf16[1024,4480]{1,0:T(8,128)(2,1)} %all-gather.4.cloned.1.call-done, bf16[2048,32]{1,0:T(8,128)(2,1)S(1)} %copy-done.17, f32[2048,1024]{1,0:T(8,128)} %fusion.19, f32[2048,1024]{1,0:T(8,128)} %fusion.15), kind=kOutput, calls=%fused_computation.39 | convolution fusion | flops 146798592 | bytes 29765632 | tf_op jit(solution)/shard_map/dot_general | solution.py:34
  609.0 3.8 fusion.11
  612.8 15.3 %fusion.13 = bf16[2048,1024]{1,0:T(8,128)(2,1)} fusion(bf16[2048,1024]{1,0:T(8,128)(2,1)S(1)} %copy-done.10, bf16[2048,1024]{0,1:T(8,128)(2,1)} %all-gather.6.cloned.1.call-done, f32[2048,2048]{1,0:T(8,128)} %get-tuple-element.51, f32[2048]{0:T(1024)S(1)} %copy-done.28, f32[2048]{0:T(1024)S(1)} %copy-done.30), kind=kOutput, calls=%fused_computation.38 | convolution fusion | flops 8608808960 | bytes 29376512 | tf_op jit(solution)/shard_map/dot_general | solution.py:30
  628.1 1.6 convert_element_type.123
  629.7 96.2 %reduce-scatter.6.cloned.1.call-done = bf16[32,2336]{1,0:T(8,128)(2,1)} async-done(((bf16[1024,2336]{1,0:T(8,128)(2,1)}), bf16[32,2336]{1,0:T(8,128)(2,1)}) %reduce-scatter.6.cloned.1.call-update) | async-done | bytes 149520 | tf_op jit(solution)/shard_map/reduce_scatter | solution.py:350
  726.0 2.0 multiply_reduce_fusion.6
  728.0 0.5 convert_divide_fusion
  (110 shorter events, 2.0 us)
Async XLA Ops:
  7.2 87.6 %all-gather.4.cloned.1.call-start = ((), (), s32[]{:S(2)}) async-start(), calls=%async_computation.3 | async-start | bytes 9461760 | tf_op jit(solution)/shard_map/all_gather | solution.py:243
  10.6 228.0 %all-gather.6.cloned.1.call-start = ((), (), s32[]{:S(2)}) async-start(), calls=%async_computation.4 | async-start | bytes 4325376 | tf_op jit(solution)/shard_map/all_gather | solution.py:265
  17.6 0.6 copy-start.31
  18.2 96.2 %copy-start.32 = (f32[32]{0:T(128)}, f32[32]{0:T(128)S(1)}, u32[]{:S(2)}) copy-start(f32[32]{0:T(128)S(1)} %get-tuple-element.63) | copy-start | bytes 388
  96.4 531.7 %reduce-scatter.8.cloned.1.call-start = ((), (), s32[]{:S(2)}) async-start(), calls=%async_computation.7 | async-start | bytes 4325376 | tf_op jit(solution)/shard_map/reduce_scatter | solution.py:301
  97.0 27.5 %copy-start.19 = (f32[2304]{0:T(1024)}, f32[2304]{0:T(1024)S(1)}, u32[]{:S(2)}) copy-start(f32[2304]{0:T(1024)S(1)} %mul.293) | copy-start | bytes 27652
  97.1 27.4 %copy-start.21 = (f32[2304]{0:T(1024)}, f32[2304]{0:T(1024)S(1)}, u32[]{:S(2)}) copy-start(f32[2304]{0:T(1024)S(1)} %mul.290) | copy-start | bytes 27652
  97.1 27.3 %copy-start.23 = (f32[2304]{0:T(1024)}, f32[2304]{0:T(1024)S(1)}, u32[]{:S(2)}) copy-start(f32[2304]{0:T(1024)S(1)} %mul.287) | copy-start | bytes 27652
  97.2 27.2 %copy-start.25 = (f32[2304]{0:T(1024)}, f32[2304]{0:T(1024)S(1)}, u32[]{:S(2)}) copy-start(f32[2304]{0:T(1024)S(1)} %mul.279) | copy-start | bytes 27652
  97.3 17.0 %copy-start.7 = (bf16[2048,1024]{1,0:T(8,128)(2,1)S(1)}, bf16[2048,1024]{1,0:T(8,128)(2,1)}, u32[]{:S(2)}) copy-start(bf16[2048,1024]{1,0:T(8,128)(2,1)} %param.11) | copy-start | bytes 12582916
  121.1 40.1 %copy-start.1 = (f32[8,256,32]{1,2,0:T(8,128)}, f32[8,256,32]{1,2,0:T(8,128)S(1)}, u32[]{:S(2)}) copy-start(f32[8,256,32]{1,2,0:T(8,128)S(1)} %copy.104) | copy-start | bytes 786436
  121.2 136.0 %copy-start.27 = (f32[2048]{0:T(1024)}, f32[2048]{0:T(1024)S(1)}, u32[]{:S(2)}) copy-start(f32[2048]{0:T(1024)S(1)} %reshape.162) | copy-start | bytes 24580
  161.2 39.9 %copy-start.8 = (bf16[2048,1024]{1,0:T(8,128)(2,1)S(1)}, bf16[2048,1024]{1,0:T(8,128)(2,1)}, u32[]{:S(2)}) copy-start(bf16[2048,1024]{1,0:T(8,128)(2,1)} %param.11) | copy-start | bytes 12582916
  199.1 2.0 copy-start.5
  201.1 22.3 %copy-start.14 = (bf16[2048,1024]{1,0:T(8,128)(2,1)S(1)}, bf16[2048,1024]{1,0:T(8,128)(2,1)}, u32[]{:S(2)}) copy-start(bf16[2048,1024]{1,0:T(8,128)(2,1)} %param.21) | copy-start | bytes 12582916
  223.4 33.7 %copy-start.29 = (f32[2048]{0:T(1024)}, f32[2048]{0:T(1024)S(1)}, u32[]{:S(2)}) copy-start(f32[2048]{0:T(1024)S(1)} %add_rsqrt_fusion) | copy-start | bytes 24580
  238.5 391.2 %reduce-scatter.4.cloned.1.call-start = ((), (), s32[]{:S(2)}) async-start(), calls=%async_computation.5 | async-start | bytes 4325376 | tf_op jit(solution)/shard_map/reduce_scatter | solution.py:314
  257.1 31.2 %copy-start.2 = (f32[8,256,32]{1,2,0:T(8,128)S(1)}, f32[8,256,32]{1,2,0:T(8,128)}, u32[]{:S(2)}) copy-start(f32[8,256,32]{1,2,0:T(8,128)} %copy-done.1) | copy-start | bytes 786436
  257.1 31.2 %copy-start.6 = (bf16[8,128,2048]{2,1,0:T(8,128)(2,1)S(1)}, bf16[8,128,2048]{2,1,0:T(8,128)(2,1)}, u32[]{:S(2)}) copy-start(bf16[8,128,2048]{2,1,0:T(8,128)(2,1)} %copy-done.5) | copy-start | bytes 12582916
  409.7 1.0 copy-start
  410.6 0.7 copy-start.3
  411.3 0.8 copy-start.4
  412.1 10.9 %copy-start.11 = (f32[8,256,32]{2,1,0:T(8,128)S(1)}, f32[8,256,32]{2,1,0:T(8,128)}, u32[]{:S(2)}) copy-start(f32[8,256,32]{2,1,0:T(8,128)} %copy.112) | copy-start | bytes 786436
  412.1 10.9 %copy-start.33 = (f32[32]{0:T(128)S(1)}, f32[32]{0:T(128)}, u32[]{:S(2)}) copy-start(f32[32]{0:T(128)} %copy-done.32) | copy-start | bytes 388
  425.7 0.8 copy-start.16
  445.1 280.9 %reduce-scatter.6.cloned.1.call-start = ((), (), s32[]{:S(2)}) async-start(), calls=%async_computation.6 | async-start | bytes 5136384 | tf_op jit(solution)/shard_map/reduce_scatter | solution.py:350
  445.1 45.7 %copy-start.20 = (f32[2304]{0:T(1024)S(1)}, f32[2304]{0:T(1024)}, u32[]{:S(2)}) copy-start(f32[2304]{0:T(1024)} %copy-done.19) | copy-start | bytes 27652
  445.1 45.7 %copy-start.22 = (f32[2304]{0:T(1024)S(1)}, f32[2304]{0:T(1024)}, u32[]{:S(2)}) copy-start(f32[2304]{0:T(1024)} %copy-done.21) | copy-start | bytes 27652
  445.1 45.7 %copy-start.24 = (f32[2304]{0:T(1024)S(1)}, f32[2304]{0:T(1024)}, u32[]{:S(2)}) copy-start(f32[2304]{0:T(1024)} %copy-done.23) | copy-start | bytes 27652
  445.1 45.7 %copy-start.26 = (f32[2304]{0:T(1024)S(1)}, f32[2304]{0:T(1024)}, u32[]{:S(2)}) copy-start(f32[2304]{0:T(1024)} %copy-done.25) | copy-start | bytes 27652
  490.9 25.1 %copy-start.9 = (bf16[2048,1024]{1,0:T(8,128)(2,1)S(1)}, bf16[2048,1024]{1,0:T(8,128)(2,1)}, u32[]{:S(2)}) copy-start(bf16[2048,1024]{1,0:T(8,128)(2,1)} %param.11) | copy-start | bytes 12582916
  515.9 10.8 %copy-start.12 = (bf16[2,1024,2304]{2,1,0:T(8,128)(2,1)}, bf16[2,1024,2304]{2,1,0:T(8,128)(2,1)S(1)}, u32[]{:S(2)}) copy-start(bf16[2,1024,2304]{2,1,0:T(8,128)(2,1)S(1)} %add_convert_fusion) | copy-start | bytes 28311556
  572.2 14.6 %copy-start.13 = (bf16[2,1024,2304]{2,1,0:T(8,128)(2,1)S(1)}, bf16[2,1024,2304]{2,1,0:T(8,128)(2,1)}, u32[]{:S(2)}) copy-start(bf16[2,1024,2304]{2,1,0:T(8,128)(2,1)} %copy-done.12) | copy-start | bytes 28311556
  586.8 14.7 %copy-start.10 = (bf16[2048,1024]{1,0:T(8,128)(2,1)S(1)}, bf16[2048,1024]{1,0:T(8,128)(2,1)}, u32[]{:S(2)}) copy-start(bf16[2048,1024]{1,0:T(8,128)(2,1)} %param.11) | copy-start | bytes 12582916
  586.8 14.7 %copy-start.17 = (bf16[2048,32]{1,0:T(8,128)(2,1)S(1)}, bf16[2048,32]{1,0:T(8,128)(2,1)}, u32[]{:S(2)}) copy-start(bf16[2048,32]{1,0:T(8,128)(2,1)} %copy-done.16) | copy-start | bytes 393220
  601.5 7.4 %copy-start.15 = (bf16[2048,1024]{1,0:T(8,128)(2,1)S(1)}, bf16[2048,1024]{1,0:T(8,128)(2,1)}, u32[]{:S(2)}) copy-start(bf16[2048,1024]{1,0:T(8,128)(2,1)} %param.21) | copy-start | bytes 12582916
  609.0 3.8 copy-start.28
  609.0 3.8 copy-start.30
  612.8 113.2 %copy-start.18 = (bf16[32,4384]{1,0:T(8,128)(2,1)S(1)}, bf16[32,4384]{1,0:T(8,128)(2,1)}, u32[]{:S(2)}) copy-start(bf16[32,4384]{1,0:T(8,128)(2,1)} %param.12) | copy-start | bytes 841732
  612.8 115.2 %copy-start.34 = (bf16[32]{0:T(256)(128)(2,1)S(1)}, bf16[32]{0:T(256)(128)(2,1)}, u32[]{:S(2)}) copy-start(bf16[32]{0:T(256)(128)(2,1)} %param.16) | copy-start | bytes 196
Sparse Core Ops, SparseCore 0:
  11.4 83.2 all-gather.3
  97.6 60.6 all-gather.5
  238.6 139.9 reduce-scatter.7
  445.2 139.9 reduce-scatter.3
  587.3 138.6 reduce-scatter.5
